TPU v7x, 32 devices: a whole 2x2x4 slice. The times are simulated.
32 devices in a mesh: wa: 4 (over z), facet: 8 (over y, x, core).
Axes of the slice: x: 2, y: 2, z: 4, core: 2. Of those that a mesh axis runs over, the one named last changes fastest.
Arguments:
- visibilities: bfloat16 [4096, 2, 64], P(('wa', 'facet')), may hold values from -6 to 6
- uv_angles: float32 [4096, 2, 64], P(('wa', 'facet')), may hold values from -3.140625 to 3.140625
- routes: int32 [4096, 1], P(('wa', 'facet')), may hold values from 0 to 31; in each aligned block of 128 rows (0 to 127, 128 to 255, ...) at most 8 rows name the same one
- offsets: int32 [4096, 2], P(('wa', 'facet')), may hold values from 0 to 448
- pixel_phase: float32 [8, 512, 512], P('facet'), may hold values from -3.140625 to 3.140625
Outputs:
- partial_images: float32 [4, 8, 512, 1024], P('wa', 'facet')
Inputs may be any that keep to these rules, and one draw needn't show every extreme that they name: `routes`: the subgrids of one device name each owner at most 8 times; some owner is named exactly 8 times.
All inputs are finite; a program needn't handle non-finite values.
Results may differ from a plain program's by a relative error of at most 0.0076.
Values may be sent and summed in bfloat16 or wider, within the bound.
No kernel may reach another device: no remote copies, remote signals or barrier semaphores. Data moves between devices by JAX's collectives and lax.ppermute only.
A program may use at most 64 MiB of HBM per device.

v0:
```python
import math

import jax
import jax.numpy as jnp
from jax import lax
from jax.sharding import PartitionSpec as P

SUB = 64
GRID = 512


def from_behind(value, axis, by):
    devices = lax.axis_size(axis)
    pairs = [(i, i + by) for i in range(devices) if 0 <= i + by < devices]
    return lax.ppermute(value, axis, pairs)


def form_subgrids(vis_block, angle_block, sub_n):
    centred = (jnp.arange(sub_n) - sub_n // 2).astype(jnp.float32)
    count_vis = vis_block.shape[2]
    norm_scale = 1.0 / math.sqrt(count_vis)
    phase_u = centred[None, :, None] * angle_block[:, 0][:, None, :]
    phase_v = centred[None, :, None] * angle_block[:, 1][:, None, :]
    cos_u = jnp.cos(phase_u)
    sin_u = jnp.sin(phase_u)
    cos_v = jnp.cos(phase_v)
    sin_v = jnp.sin(phase_v)
    vis_re = vis_block[:, 0].astype(jnp.float32)[:, None, :]
    vis_im = vis_block[:, 1].astype(jnp.float32)[:, None, :]
    left_re = (cos_u * vis_re - sin_u * vis_im) * norm_scale
    left_im = (cos_u * vis_im + sin_u * vis_re) * norm_scale
    left_side = jnp.concatenate([left_re, left_im], axis=2).astype(jnp.bfloat16)
    right_side = jnp.concatenate(
        [jnp.concatenate([cos_v, -sin_v], axis=2), jnp.concatenate([sin_v, cos_v], axis=2)], axis=1
    ).astype(jnp.bfloat16)
    return jnp.einsum(
        "bak,bck->bac", left_side, right_side, preferred_element_type=jnp.float32
    ).astype(jnp.bfloat16)


def form_many(vis_all, angle_all, sub_n):
    total = vis_all.shape[0]
    count_vis = vis_all.shape[2]
    block_n = math.gcd(total, 8)
    vis_blocks = vis_all.reshape(total // block_n, block_n, 2, count_vis)
    angle_blocks = angle_all.reshape(total // block_n, block_n, 2, count_vis)
    formed = lax.map(
        lambda items: form_subgrids(items[0], items[1], sub_n), (vis_blocks, angle_blocks)
    )
    return formed.reshape(total, sub_n, 2 * sub_n)


def place_grid(sub_data, sub_offsets, sub_n, grid_n):
    slot_count = sub_data.shape[0]
    block_n = math.gcd(slot_count, 16)
    col_base = jnp.arange(2 * sub_n, dtype=jnp.int32)
    col_shift = col_base // sub_n * grid_n + col_base % sub_n
    targets = jnp.arange(2 * grid_n, dtype=jnp.int32)
    sub_line = jnp.arange(sub_n, dtype=jnp.int32)
    data_blocks = sub_data.reshape(slot_count // block_n, block_n, sub_n, 2 * sub_n)
    offset_blocks = sub_offsets.reshape(slot_count // block_n, block_n, 2)

    def add_piece(running_grid, items):
        piece_data, piece_offsets = items
        place_table = (
            col_shift[None, :, None] + piece_offsets[:, 1][:, None, None] == targets[None, None, :]
        ).astype(jnp.bfloat16)
        placed = jnp.einsum(
            "bcd,bdj->bcj", piece_data, place_table, preferred_element_type=jnp.float32
        )
        row_targets = (piece_offsets[:, 0][:, None] + sub_line[None, :]).reshape(-1)
        running_grid = running_grid.at[row_targets].add(placed.reshape(-1, 2 * grid_n))
        return (running_grid, None)

    start_grid = jnp.zeros((grid_n, 2 * grid_n), jnp.float32)
    final_grid, _ = lax.scan(add_piece, start_grid, (data_blocks, offset_blocks))
    return final_grid


def dft_tables(grid_n):
    index_line = jnp.arange(grid_n, dtype=jnp.int32)
    product = index_line[:, None] * index_line[None, :] % grid_n
    angle_table = product.astype(jnp.float32) * (2.0 * math.pi / grid_n)
    root_scale = 1.0 / math.sqrt(grid_n)
    cos_table = jnp.cos(angle_table) * root_scale
    sin_table = jnp.sin(angle_table) * root_scale
    row_table = jnp.concatenate([cos_table, sin_table], axis=0).astype(jnp.bfloat16)
    col_table = jnp.concatenate(
        [
            jnp.concatenate([cos_table, sin_table], axis=1),
            jnp.concatenate([-sin_table, cos_table], axis=1),
        ],
        axis=0,
    ).astype(jnp.bfloat16)
    return (row_table, col_table)


def inverse_dft(grid_bf, row_table, col_table, grid_n):
    stacked = jnp.dot(row_table, grid_bf, preferred_element_type=jnp.float32)
    half_re = stacked[:grid_n, :grid_n] - stacked[grid_n:, grid_n:]
    half_im = stacked[:grid_n, grid_n:] + stacked[grid_n:, :grid_n]
    half_band = jnp.concatenate([half_re, half_im], axis=1).astype(jnp.bfloat16)
    return jnp.dot(half_band, col_table, preferred_element_type=jnp.float32)


def phase_times(phase_re, phase_im, field, grid_n):
    field_re = field[..., :grid_n]
    field_im = field[..., grid_n:]
    return jnp.concatenate(
        [phase_re * field_re - phase_im * field_im, phase_re * field_im + phase_im * field_re],
        axis=-1,
    )


def on_device(visibilities, uv_angles, routes, offsets, pixel_phase):
    sub_count = visibilities.shape[0]
    count_vis = visibilities.shape[2]
    wa_count = lax.axis_size("wa")
    facet_count = lax.axis_size("facet")
    owners_n = wa_count * facet_count
    capacity = max(2, (2 * sub_count + owners_n - 1) // owners_n)
    slots_n = owners_n * capacity
    owner_index = routes[:, 0]
    one_hot = (owner_index[:, None] == jnp.arange(owners_n, dtype=jnp.int32)[None, :]).astype(
        jnp.int32
    )
    slot_rank = jnp.sum(jnp.cumsum(one_hot, axis=0) * one_hot, axis=1) - 1
    slot_index = owner_index * capacity + slot_rank
    send_offsets = jnp.zeros((slots_n, 2), jnp.int32).at[slot_index].set(offsets)
    send_vis = (
        jnp.zeros((slots_n, 2, count_vis), jnp.float32)
        .at[slot_index]
        .set(visibilities.astype(jnp.float32))
    )
    send_angles = jnp.zeros((slots_n, 2, count_vis), jnp.float32).at[slot_index].set(uv_angles)
    got_vis, got_angles, got_offsets = (
        lax.all_to_all(
            send_vis.reshape(owners_n, capacity, 2, count_vis),
            ("wa", "facet"),
            split_axis=0,
            concat_axis=0,
            tiled=True,
        ),
        lax.all_to_all(
            send_angles.reshape(owners_n, capacity, 2, count_vis),
            ("wa", "facet"),
            split_axis=0,
            concat_axis=0,
            tiled=True,
        ),
        lax.all_to_all(
            send_offsets.reshape(owners_n, capacity, 2),
            ("wa", "facet"),
            split_axis=0,
            concat_axis=0,
            tiled=True,
        ),
    )
    got_vis = got_vis.reshape(slots_n, 2, count_vis).astype(jnp.bfloat16)
    got_angles = got_angles.reshape(slots_n, 2, count_vis)
    got_data = form_many(got_vis, got_angles, SUB)
    got_offsets = got_offsets.reshape(slots_n, 2)
    facet_grid = place_grid(got_data, got_offsets, SUB, GRID).astype(jnp.bfloat16)
    row_table, col_table = dft_tables(GRID)
    image_band = inverse_dft(facet_grid, row_table, col_table, GRID)
    phase_re = jnp.cos(pixel_phase[0])
    phase_im = jnp.sin(pixel_phase[0])
    plane_index = lax.axis_index("wa")
    running = image_band
    for section in range(1, wa_count):
        incoming = from_behind(running, "wa", 1)
        candidate = phase_times(phase_re, phase_im, incoming, GRID) + image_band
        running = jnp.where(plane_index == section, candidate, running)
    return running.reshape(1, 1, GRID, 2 * GRID)


def solution(mesh):
    in_specs = (
        P(("wa", "facet"), None, None),
        P(("wa", "facet"), None, None),
        P(("wa", "facet"), None),
        P(("wa", "facet"), None),
        P("facet", None, None),
    )
    out_specs = P("wa", "facet", None, None)
    return jax.shard_map(
        on_device, mesh=mesh, in_specs=in_specs, out_specs=out_specs, check_vma=False
    )
```

profile of v0, /device:TPU:26, one launch (start us, length us, event | category | flops | bytes accessed | tf_op | source)
XLA Modules:
  0.0 568.4 jit_solution(15460763832588676251)
XLA Ops:
  5.0 5.9 %all-to-all-start = ((s32[32,8,2]{1,2,0:T(2,128)}), s32[32,8,2]{1,2,0:T(2,128)S(1)}, u32[]{:S(2)}, u32[]{:S(2)}) async-start(s32[32,8,2]{1,2,0:T(2,128)} %copy.16), calls=%async_computation | async-start | bytes 65536 | tf_op jit(solution)/shard_map/all_to_all | solution.py:151
  17.0 5.8 %all-to-all-start.2 = ((bf16[32,2,512]{2,1,0:T(2,128)(2,1)}), bf16[32,2,512]{2,1,0:T(2,128)(2,1)S(1)}, u32[]{:S(2)}, u32[]{:S(2)}) async-start(bf16[32,2,512]{2,1,0:T(2,128)(2,1)} %reshape.145), calls=%async_computation.2 | async-start | bytes 131072 | tf_op jit(solution)/shard_map/all_to_all | solution.py:137
  28.2 5.8 %all-to-all-start.1 = ((f32[32,1,1024]{2,1,0:T(1,128)}), f32[32,1,1024]{2,1,0:T(1,128)S(1)}, u32[]{:S(2)}, u32[]{:S(2)}) async-start(f32[32,1,1024]{2,1,0:T(1,128)} %reshape.143), calls=%async_computation.1 | async-start | bytes 262144 | tf_op jit(solution)/shard_map/all_to_all | solution.py:144
  44.9 101.1 %while.23 = (s32[]{:T(128)}, bf16[32,8,64,128]{3,2,1,0:T(8,128)(2,1)}, f32[32,8,2,64]{3,1,2,0:T(8,128)S(1)}, bf16[32,8,2,64]{3,1,2,0:T(8,128)(2,1)S(1)}, s32[]{:T(128)}) while((s32[]{:T(128)}, bf16[32,8,64,128]{3,2,1,0:T(8,128)(2,1)}, f32[32,8,2,64]{3,1,2,0:T(8,128)S(1)}, bf16[32,8,2,64]{3,1,2,0:T(8,128)(2,1)S(1)}, s32[]{:T(128)}) %tuple.76), condition=%wide.region_5.6_spmd, body=%wide.region_4.5_spmd.sunk | while | flops 18678912 | bytes 822341 | solution.py:47
  146.3 257.3 %while.24 = (s32[]{:T(128)}, f32[512,1024]{1,0:T(8,128)S(1)}, s32[16,16,2]{1,0,2:T(8,128)S(1)}, bf16[16,16,64,128]{3,2,1,0:T(8,128)(2,1)}, s32[]{:T(128)}) while((s32[]{:T(128)}, f32[512,1024]{1,0:T(8,128)S(1)}, s32[16,16,2]{1,0,2:T(8,128)S(1)}, bf16[16,16,64,128]{3,2,1,0:T(8,128)(2,1)}, s32[]{:T(128)}) %tuple.74), condition=%wide.region_9.10_spmd.clone, body=%wide.region_7.9_spmd.clone.sunk | while | flops 271589120 | bytes 17082560 | solution.py:76
  151.3 11.1 %scatter_fusion = f32[512,1024]{1,0:T(8,128)S(1)} fusion(f32[512,1024]{1,0:T(8,128)S(1)} %get-tuple-element.256, s32[1024]{0:T(1024)S(1)} %bitcast.121, f32[1024,1024]{1,0:T(8,128)} %bitcast.115), kind=kCustom, calls=%fused_computation.clone.clone.1 | custom fusion | flops 1048576 | bytes 12587008 | tf_op jit(solution)/shard_map/while/body/eval_jaxpr/scatter-add | solution.py:72
  162.5 4.7 fusion.98
  167.3 11.1 %scatter_fusion = f32[512,1024]{1,0:T(8,128)S(1)} fusion(f32[512,1024]{1,0:T(8,128)S(1)} %get-tuple-element.256, s32[1024]{0:T(1024)S(1)} %bitcast.121, f32[1024,1024]{1,0:T(8,128)} %bitcast.115), kind=kCustom, calls=%fused_computation.clone.clone.1 | custom fusion | flops 1048576 | bytes 12587008 | tf_op jit(solution)/shard_map/while/body/eval_jaxpr/scatter-add | solution.py:72
  183.4 11.1 %scatter_fusion = f32[512,1024]{1,0:T(8,128)S(1)} fusion(f32[512,1024]{1,0:T(8,128)S(1)} %get-tuple-element.256, s32[1024]{0:T(1024)S(1)} %bitcast.121, f32[1024,1024]{1,0:T(8,128)} %bitcast.115), kind=kCustom, calls=%fused_computation.clone.clone.1 | custom fusion | flops 1048576 | bytes 12587008 | tf_op jit(solution)/shard_map/while/body/eval_jaxpr/scatter-add | solution.py:72
  199.5 11.1 %scatter_fusion = f32[512,1024]{1,0:T(8,128)S(1)} fusion(f32[512,1024]{1,0:T(8,128)S(1)} %get-tuple-element.256, s32[1024]{0:T(1024)S(1)} %bitcast.121, f32[1024,1024]{1,0:T(8,128)} %bitcast.115), kind=kCustom, calls=%fused_computation.clone.clone.1 | custom fusion | flops 1048576 | bytes 12587008 | tf_op jit(solution)/shard_map/while/body/eval_jaxpr/scatter-add | solution.py:72
  210.7 4.7 fusion.98
  215.6 11.1 %scatter_fusion = f32[512,1024]{1,0:T(8,128)S(1)} fusion(f32[512,1024]{1,0:T(8,128)S(1)} %get-tuple-element.256, s32[1024]{0:T(1024)S(1)} %bitcast.121, f32[1024,1024]{1,0:T(8,128)} %bitcast.115), kind=kCustom, calls=%fused_computation.clone.clone.1 | custom fusion | flops 1048576 | bytes 12587008 | tf_op jit(solution)/shard_map/while/body/eval_jaxpr/scatter-add | solution.py:72
  231.7 11.1 %scatter_fusion = f32[512,1024]{1,0:T(8,128)S(1)} fusion(f32[512,1024]{1,0:T(8,128)S(1)} %get-tuple-element.256, s32[1024]{0:T(1024)S(1)} %bitcast.121, f32[1024,1024]{1,0:T(8,128)} %bitcast.115), kind=kCustom, calls=%fused_computation.clone.clone.1 | custom fusion | flops 1048576 | bytes 12587008 | tf_op jit(solution)/shard_map/while/body/eval_jaxpr/scatter-add | solution.py:72
  242.9 4.7 fusion.98
  247.7 11.1 %scatter_fusion = f32[512,1024]{1,0:T(8,128)S(1)} fusion(f32[512,1024]{1,0:T(8,128)S(1)} %get-tuple-element.256, s32[1024]{0:T(1024)S(1)} %bitcast.121, f32[1024,1024]{1,0:T(8,128)} %bitcast.115), kind=kCustom, calls=%fused_computation.clone.clone.1 | custom fusion | flops 1048576 | bytes 12587008 | tf_op jit(solution)/shard_map/while/body/eval_jaxpr/scatter-add | solution.py:72
  263.8 11.1 %scatter_fusion = f32[512,1024]{1,0:T(8,128)S(1)} fusion(f32[512,1024]{1,0:T(8,128)S(1)} %get-tuple-element.256, s32[1024]{0:T(1024)S(1)} %bitcast.121, f32[1024,1024]{1,0:T(8,128)} %bitcast.115), kind=kCustom, calls=%fused_computation.clone.clone.1 | custom fusion | flops 1048576 | bytes 12587008 | tf_op jit(solution)/shard_map/while/body/eval_jaxpr/scatter-add | solution.py:72
  275.1 4.7 fusion.98
  279.9 11.1 %scatter_fusion = f32[512,1024]{1,0:T(8,128)S(1)} fusion(f32[512,1024]{1,0:T(8,128)S(1)} %get-tuple-element.256, s32[1024]{0:T(1024)S(1)} %bitcast.121, f32[1024,1024]{1,0:T(8,128)} %bitcast.115), kind=kCustom, calls=%fused_computation.clone.clone.1 | custom fusion | flops 1048576 | bytes 12587008 | tf_op jit(solution)/shard_map/while/body/eval_jaxpr/scatter-add | solution.py:72
  291.1 4.7 fusion.98
  296.0 11.1 %scatter_fusion = f32[512,1024]{1,0:T(8,128)S(1)} fusion(f32[512,1024]{1,0:T(8,128)S(1)} %get-tuple-element.256, s32[1024]{0:T(1024)S(1)} %bitcast.121, f32[1024,1024]{1,0:T(8,128)} %bitcast.115), kind=kCustom, calls=%fused_computation.clone.clone.1 | custom fusion | flops 1048576 | bytes 12587008 | tf_op jit(solution)/shard_map/while/body/eval_jaxpr/scatter-add | solution.py:72
  312.1 11.1 %scatter_fusion = f32[512,1024]{1,0:T(8,128)S(1)} fusion(f32[512,1024]{1,0:T(8,128)S(1)} %get-tuple-element.256, s32[1024]{0:T(1024)S(1)} %bitcast.121, f32[1024,1024]{1,0:T(8,128)} %bitcast.115), kind=kCustom, calls=%fused_computation.clone.clone.1 | custom fusion | flops 1048576 | bytes 12587008 | tf_op jit(solution)/shard_map/while/body/eval_jaxpr/scatter-add | solution.py:72
  323.3 4.7 fusion.98
  328.2 11.1 %scatter_fusion = f32[512,1024]{1,0:T(8,128)S(1)} fusion(f32[512,1024]{1,0:T(8,128)S(1)} %get-tuple-element.256, s32[1024]{0:T(1024)S(1)} %bitcast.121, f32[1024,1024]{1,0:T(8,128)} %bitcast.115), kind=kCustom, calls=%fused_computation.clone.clone.1 | custom fusion | flops 1048576 | bytes 12587008 | tf_op jit(solution)/shard_map/while/body/eval_jaxpr/scatter-add | solution.py:72
  344.2 11.1 %scatter_fusion = f32[512,1024]{1,0:T(8,128)S(1)} fusion(f32[512,1024]{1,0:T(8,128)S(1)} %get-tuple-element.256, s32[1024]{0:T(1024)S(1)} %bitcast.121, f32[1024,1024]{1,0:T(8,128)} %bitcast.115), kind=kCustom, calls=%fused_computation.clone.clone.1 | custom fusion | flops 1048576 | bytes 12587008 | tf_op jit(solution)/shard_map/while/body/eval_jaxpr/scatter-add | solution.py:72
  355.5 4.7 fusion.98
  360.3 11.1 %scatter_fusion = f32[512,1024]{1,0:T(8,128)S(1)} fusion(f32[512,1024]{1,0:T(8,128)S(1)} %get-tuple-element.256, s32[1024]{0:T(1024)S(1)} %bitcast.121, f32[1024,1024]{1,0:T(8,128)} %bitcast.115), kind=kCustom, calls=%fused_computation.clone.clone.1 | custom fusion | flops 1048576 | bytes 12587008 | tf_op jit(solution)/shard_map/while/body/eval_jaxpr/scatter-add | solution.py:72
  371.5 4.7 fusion.98
  376.4 11.1 %scatter_fusion = f32[512,1024]{1,0:T(8,128)S(1)} fusion(f32[512,1024]{1,0:T(8,128)S(1)} %get-tuple-element.256, s32[1024]{0:T(1024)S(1)} %bitcast.121, f32[1024,1024]{1,0:T(8,128)} %bitcast.115), kind=kCustom, calls=%fused_computation.clone.clone.1 | custom fusion | flops 1048576 | bytes 12587008 | tf_op jit(solution)/shard_map/while/body/eval_jaxpr/scatter-add | solution.py:72
  392.5 11.1 %scatter_fusion = f32[512,1024]{1,0:T(8,128)S(1)} fusion(f32[512,1024]{1,0:T(8,128)S(1)} %get-tuple-element.256, s32[1024]{0:T(1024)S(1)} %bitcast.121, f32[1024,1024]{1,0:T(8,128)} %bitcast.115), kind=kCustom, calls=%fused_computation.clone.clone.1 | custom fusion | flops 1048576 | bytes 12587008 | tf_op jit(solution)/shard_map/while/body/eval_jaxpr/scatter-add | solution.py:72
  413.4 43.5 %collective-permute-done = f32[512,1024]{1,0:T(8,128)} collective-permute-done((f32[512,1024]{1,0:T(8,128)S(1)}, f32[512,1024]{1,0:T(8,128)}, u32[]{:S(2)}, u32[]{:S(2)}) %collective-permute-start) | collective-permute-done | bytes 2097184 | tf_op jit(solution)/shard_map/ppermute | solution.py:15
  462.0 47.8 %collective-permute-done.1 = f32[512,1024]{1,0:T(8,128)} collective-permute-done((f32[512,1024]{1,0:T(8,128)}, f32[512,1024]{1,0:T(8,128)}, u32[]{:S(2)}, u32[]{:S(2)}) %collective-permute-start.1) | collective-permute-done | bytes 2097184 | tf_op jit(solution)/shard_map/ppermute | solution.py:15
  517.1 46.8 %collective-permute-done.2 = f32[512,1024]{1,0:T(8,128)} collective-permute-done((f32[512,1024]{1,0:T(8,128)}, f32[512,1024]{1,0:T(8,128)}, u32[]{:S(2)}, u32[]{:S(2)}) %collective-permute-start.2) | collective-permute-done | bytes 2097184 | tf_op jit(solution)/shard_map/ppermute | solution.py:15
  (393 shorter events, 196.4 us)
Async XLA Ops:
  0.0 22.8 %copy-start.2 = (f32[128,2,64]{0,2,1:T(8,128)S(1)}, f32[128,2,64]{0,2,1:T(8,128)}, u32[]{:S(2)}) copy-start(f32[128,2,64]{0,2,1:T(8,128)} %param.10) | copy-start | bytes 196612
  5.0 11.9 %all-to-all-start = ((s32[32,8,2]{1,2,0:T(2,128)}), s32[32,8,2]{1,2,0:T(2,128)S(1)}, u32[]{:S(2)}, u32[]{:S(2)}) async-start(s32[32,8,2]{1,2,0:T(2,128)} %copy.16), calls=%async_computation | async-start | bytes 65536 | tf_op jit(solution)/shard_map/all_to_all | solution.py:151
  17.0 11.2 %all-to-all-start.2 = ((bf16[32,2,512]{2,1,0:T(2,128)(2,1)}), bf16[32,2,512]{2,1,0:T(2,128)(2,1)S(1)}, u32[]{:S(2)}, u32[]{:S(2)}) async-start(bf16[32,2,512]{2,1,0:T(2,128)(2,1)} %reshape.145), calls=%async_computation.2 | async-start | bytes 131072 | tf_op jit(solution)/shard_map/all_to_all | solution.py:137
  28.2 15.1 %all-to-all-start.1 = ((f32[32,1,1024]{2,1,0:T(1,128)}), f32[32,1,1024]{2,1,0:T(1,128)S(1)}, u32[]{:S(2)}, u32[]{:S(2)}) async-start(f32[32,1,1024]{2,1,0:T(1,128)} %reshape.143), calls=%async_computation.1 | async-start | bytes 262144 | tf_op jit(solution)/shard_map/all_to_all | solution.py:144
  404.9 1.0 copy-start.1
  407.2 49.7 %collective-permute-start = (f32[512,1024]{1,0:T(8,128)S(1)}, f32[512,1024]{1,0:T(8,128)}, u32[]{:S(2)}, u32[]{:S(2)}) collective-permute-start(f32[512,1024]{1,0:T(8,128)S(1)} %fusion.42), channel_id=1, source_target_pairs={{0,8},{8,16},{16,24},{1,9},{9,17},{17,25},{2,10},{10,18},{18,26},{... | collective-permute-start | bytes 6291464 | tf_op jit(solution)/shard_map/ppermute | solution.py:15
  413.4 45.5 %copy-start = (f32[1,512,512]{2,1,0:T(8,128)}, f32[1,512,512]{2,1,0:T(8,128)S(1)}, u32[]{:S(2)}) copy-start(f32[1,512,512]{2,1,0:T(8,128)S(1)} %get-tuple-element.160) | copy-start | bytes 3145732
  460.7 49.1 %collective-permute-start.1 = (f32[512,1024]{1,0:T(8,128)}, f32[512,1024]{1,0:T(8,128)}, u32[]{:S(2)}, u32[]{:S(2)}) collective-permute-start(f32[512,1024]{1,0:T(8,128)} %add_select_fusion), channel_id=1, source_target_pairs={{0,8},{8,16},{16,24},{1,9},{9,17},{17,25},{2,10},{10,18},{18,26},{... | collective-permute-start | bytes 6291464 | tf_op jit(solution)/shard_map/ppermute | solution.py:15
  515.8 48.1 %collective-permute-start.2 = (f32[512,1024]{1,0:T(8,128)}, f32[512,1024]{1,0:T(8,128)}, u32[]{:S(2)}, u32[]{:S(2)}) collective-permute-start(f32[512,1024]{1,0:T(8,128)} %fusion.50), channel_id=1, source_target_pairs={{0,8},{8,16},{16,24},{1,9},{9,17},{17,25},{2,10},{10,18},{18,26},{... | collective-permute-start | bytes 6291464 | tf_op jit(solution)/shard_map/ppermute | solution.py:15
where the time goes:
time: 572 us; the launch traced here: 568 us
  other arithmetic  276 us (48%)
  waiting for transfers between devices  138 us (24%)
  matrix products  110 us (19%)
  local copies, waits for them, and re-layouts  22.2 us (4%)
  starting transfers between devices  21.6 us (4%)
    scatter-add x16, other arithmetic, add_piece(): running_grid.at[row_targets].add(placed.reshape(-1, 2 * grid_n))  177 us
    ppermute x3, waiting for transfers between devices, from_behind(): return lax.ppermute(value, axis, pairs)  138 us
    another operation x35, other arithmetic  77.7 us
    dot_general x16, matrix products, add_piece(): jnp.einsum('bcd,bdj->bcj', piece_data, place_table, preferred_element_typ...  75.1 us
    dot_general x32, matrix products, form_subgrids(): jnp.einsum('bak,bck->bac', left_side, right_side, preferred_element_type=...  31.8 us
  transfers between devices with their start and end apart: 6, of which 3 were waited for; matrix products, arithmetic and copies ran while one was open for 4% of the time, Pallas kernels for 0%

commit v1 on v0

v1 whole, which is shorter than its diff:
```python
import functools
import math

import jax
import jax.numpy as jnp
import numpy as np
from jax import lax
from jax.experimental import pallas as pl
from jax.experimental.pallas import tpu as pltpu
from jax.sharding import PartitionSpec as P

SUB = 64
LANES = 128
ROWS = 8
GROUP = 8
CHUNKS = 4
SINE = tuple(
    float(v)
    for v in np.linalg.lstsq(
        *(
            lambda x, w: (
                (x[:, None] ** np.arange(1, 14, 2)[None, :]) * w[:, None],
                np.sin(2 * np.pi * x) * w,
            )
        )(
            0.5 * np.cos(np.pi * (np.arange(2000) + 0.5) / 4000),
            np.ones(2000),
        ),
        rcond=None,
    )[0]
)


def sine_turns(turns):
    x = turns - jnp.round(turns)
    x2 = x * x
    total = jnp.full_like(x, SINE[-1])
    for c in SINE[-2::-1]:
        total = total * x2 + c
    return total * x


def pack_kernel(owners, cap, routes, offsets, angles, vis, out, counts):
    out[...] = jnp.zeros_like(out)

    def clear(i, _):
        counts[i] = 0
        return 0

    lax.fori_loop(0, owners, clear, 0)
    lane = lax.broadcasted_iota(jnp.int32, (1, LANES), 1)

    def place(i, _):
        owner = routes[i]
        rank = counts[owner]
        counts[owner] = rank + 1
        base = owner * (3 * cap) + rank
        out[pl.ds(base, 1), :] = angles[pl.ds(i, 1), :]
        out[pl.ds(base + cap, 1), :] = vis[pl.ds(i, 1), :]
        first, second = offsets[2 * i], offsets[2 * i + 1]
        meta = jnp.where(lane == 0, first, jnp.where(lane == 1, second, 0))
        out[pl.ds(base + 2 * cap, 1), :] = meta.astype(jnp.float32)
        return 0

    lax.fori_loop(0, angles.shape[0], place, 0, unroll=4)


def pack(routes, offsets, angles, vis, owners, cap):
    smem = pl.BlockSpec(memory_space=pltpu.SMEM)
    vmem = pl.BlockSpec(memory_space=pltpu.VMEM)
    return pl.pallas_call(
        functools.partial(pack_kernel, owners, cap),
        out_shape=jax.ShapeDtypeStruct((owners * cap * 3, LANES), jnp.float32),
        in_specs=[smem, smem, vmem, vmem],
        out_specs=vmem,
        scratch_shapes=[pltpu.SMEM((owners,), jnp.int32)],
        name="pack",
    )(routes, offsets, angles, vis)


def image_kernel(
    grid_n, offsets, angles, vis, first_hbm, second_hbm, out,
    tables, turns_u, turns_v, amp_a, amp_b, grid, dense, first, second, sems,
):
    slots = angles.shape[0]
    blocks = grid_n // SUB
    copies = [
        pltpu.make_async_copy(first_hbm, first, sems.at[0]),
        pltpu.make_async_copy(second_hbm, second, sems.at[1]),
    ]
    for copy in copies:
        copy.start()

    lane = lax.broadcasted_iota(jnp.int32, (ROWS, LANES), 1)
    low = lane < SUB
    row = lax.broadcasted_iota(jnp.int32, (ROWS, LANES), 0)
    quarter = jnp.where(low, 0.25, 0.0).astype(jnp.float32)
    sign = jnp.where(low, -1.0, 1.0).astype(jnp.float32)
    row_f = row.astype(jnp.float32)
    steps = row_f * ROWS - SUB // 2

    low_all = lax.broadcasted_iota(jnp.int32, (slots, LANES), 1) < SUB
    both = angles[...] * (1.0 / (2.0 * math.pi))
    swapped = pltpu.roll(both, SUB, 1)
    turns_u[...] = jnp.where(low_all, both, swapped)
    turns_v[...] = jnp.where(low_all, swapped, both)
    both = vis[...] * (1.0 / math.sqrt(SUB))
    swapped = pltpu.roll(both, SUB, 1)
    amp_a[...] = jnp.where(low_all, both, swapped)
    amp_b[...] = jnp.where(low_all, swapped, both)

    def clear(b, _):
        grid[b] = jnp.zeros(grid.shape[1:], grid.dtype)
        return 0

    lax.fori_loop(0, blocks + 1, clear, 0)

    def spread(ref, s):
        return jnp.broadcast_to(ref[pl.ds(s, 1), :], (ROWS, LANES))

    def prepare(s):
        off_u, off_v = offsets[2 * s], offsets[2 * s + 1]
        shift_u = off_u & (ROWS - 1)
        shift_v = off_v & (ROWS - 1)
        step_v = (off_v & (SUB - 1)) // ROWS
        tu, tv = spread(turns_u, s), spread(turns_v, s)
        a, b = spread(amp_a, s), spread(amp_b, s)
        cs = sine_turns(tu * (row - shift_u).astype(jnp.float32) + quarter)
        sc = pltpu.roll(cs, SUB, 1) * sign
        tables[s, 0] = cs * a + sc * b
        tables[s, 1] = sc * a - cs * b
        cs = sine_turns(tu * steps + quarter)
        sc = pltpu.roll(cs, SUB, 1)
        tables[s, 2] = jnp.where(low, cs, sc)
        tables[s, 3] = jnp.where(low, sc, cs)
        cs = sine_turns(tv * ((row - shift_v) & (ROWS - 1)).astype(jnp.float32) + quarter)
        tables[s, 4] = -(cs * sign)
        tables[s, 5] = pltpu.roll(cs, SUB, 1)
        turn = ((row - step_v) & (ROWS - 1)) * ROWS - SUB // 2
        cs = sine_turns(tv * turn.astype(jnp.float32) + quarter)
        sc = pltpu.roll(cs, SUB, 1)
        tables[s, 6] = jnp.where(low, cs, sc)
        tables[s, 7] = jnp.where(low, sc, cs)

    def prepare_group(g, _):
        for i in range(GROUP):
            prepare(g * GROUP + i)
        return 0

    lax.fori_loop(0, slots // GROUP, prepare_group, 0)

    def form(s):
        off_u, off_v = offsets[2 * s], offsets[2 * s + 1]
        shift_u = off_u & (ROWS - 1)
        shift_v = off_v & (ROWS - 1)

        def line(k, j):
            return jnp.broadcast_to(tables[s, k, j : j + 1, :], (ROWS, LANES))

        x, y = tables[s, 0], tables[s, 1]
        pieces = [x * line(2, j) + y * line(3, j) for j in range(SUB // ROWS)]
        last = x * line(2, 0) - y * line(3, 0)
        pieces[0] = jnp.where(row >= shift_u, pieces[0], 0.0)
        pieces.append(jnp.where(row < shift_u, last, 0.0))
        left = jnp.concatenate(pieces, axis=0).astype(jnp.bfloat16)
        x, y = tables[s, 4], tables[s, 5]
        early = row < shift_v
        re, im = [], []
        wr_before, wi_before = line(6, SUB // ROWS - 1), line(7, SUB // ROWS - 1)
        for j in range(SUB // ROWS):
            wr_now, wi_now = line(6, j), line(7, j)
            wr = jnp.where(early, wr_before, wr_now)
            wi = jnp.where(early, wi_before, wi_now)
            re.append(x * wr - y * wi)
            im.append(y * wr + x * wi)
            wr_before, wi_before = wr_now, wi_now
        right = jnp.concatenate(re + im, axis=0).astype(jnp.bfloat16)
        return lax.dot_general(
            left, right, (((1,), (1,)), ((), ())), preferred_element_type=jnp.float32
        )

    lane_cell = lax.broadcasted_iota(jnp.int32, (SUB + ROWS, LANES), 1) & (SUB - 1)

    def add(s, piece):
        off_u, off_v = offsets[2 * s], offsets[2 * s + 1]
        start = pl.multiple_of(off_u // ROWS * ROWS, ROWS)
        block = off_v // SUB
        here = lane_cell >= (off_v & (SUB - 1))
        rows = pl.ds(start, SUB + ROWS)
        grid[block, rows, :] += jnp.where(here, piece, 0.0)
        grid[block + 1, rows, :] += jnp.where(here, 0.0, piece)

    def add_group(g, _):
        formed = [form(g * GROUP + i) for i in range(GROUP)]
        for i in range(GROUP):
            add(g * GROUP + i, formed[i])
        return 0

    lax.fori_loop(0, slots // GROUP, add_group, 0)

    sign_all = jnp.where(lax.broadcasted_iota(jnp.int32, (grid_n, LANES), 1) < SUB, -1.0, 1.0)
    for b in range(blocks):
        cells = grid[b, 0:grid_n, :]
        columns = slice(b * LANES, (b + 1) * LANES)
        dense[0:grid_n, columns] = cells.astype(jnp.bfloat16)
        dense[grid_n : 2 * grid_n, columns] = (pltpu.roll(cells, SUB, 1) * sign_all).astype(
            jnp.bfloat16
        )
    for copy in copies:
        copy.wait()
    step = math.gcd(grid_n, LANES)

    def transform(i, _):
        rows = pl.ds(pl.multiple_of(i * step, step), step)
        half = jnp.dot(first[rows, :], dense[...], preferred_element_type=jnp.float32)
        out[rows, :] = jnp.dot(
            half.astype(jnp.bfloat16), second[...], preferred_element_type=jnp.float32
        )
        return 0

    lax.fori_loop(0, grid_n // step, transform, 0)


def form_image(offsets, angles, vis, first, second, grid_n):
    slots = angles.shape[0]
    blocks = grid_n // SUB
    smem = pl.BlockSpec(memory_space=pltpu.SMEM)
    vmem = pl.BlockSpec(memory_space=pltpu.VMEM)
    anywhere = pl.BlockSpec(memory_space=pl.ANY)
    line = pltpu.VMEM((slots, LANES), jnp.float32)
    return pl.pallas_call(
        functools.partial(image_kernel, grid_n),
        out_shape=jax.ShapeDtypeStruct((grid_n, 2 * grid_n), jnp.float32),
        in_specs=[smem, vmem, vmem, anywhere, anywhere],
        out_specs=vmem,
        scratch_shapes=[
            pltpu.VMEM((slots, 8, ROWS, LANES), jnp.float32),
            line, line, line, line,
            pltpu.VMEM((blocks + 1, grid_n + ROWS, LANES), jnp.float32),
            pltpu.VMEM((2 * grid_n, 2 * grid_n), jnp.bfloat16),
            pltpu.VMEM(first.shape, jnp.bfloat16),
            pltpu.VMEM(second.shape, jnp.bfloat16),
            pltpu.SemaphoreType.DMA((2,)),
        ],
        compiler_params=pltpu.CompilerParams(vmem_limit_bytes=40 * 1024 * 1024),
        name="image",
    )(offsets, angles, vis, first, second)


def dft_tables(grid_n):
    line = np.arange(grid_n)
    angle = (line[:, None] * line[None, :] % grid_n) * (2.0 * np.pi / grid_n)
    cos = np.cos(angle) / math.sqrt(grid_n)
    sin = np.sin(angle) / math.sqrt(grid_n)
    first = np.concatenate([cos, sin], axis=1)
    real = np.concatenate([cos, sin], axis=1).reshape(grid_n // SUB, SUB, 2 * grid_n)
    imag = np.concatenate([-sin, cos], axis=1).reshape(grid_n // SUB, SUB, 2 * grid_n)
    second = np.concatenate([real, imag], axis=1).reshape(2 * grid_n, 2 * grid_n)
    return first.astype(np.float32).astype(jnp.bfloat16), second.astype(np.float32).astype(jnp.bfloat16)


def on_device(visibilities, uv_angles, routes, offsets, pixel_phase):
    sub_count = visibilities.shape[0]
    count_vis = visibilities.shape[2]
    grid_n = pixel_phase.shape[1]
    planes = lax.axis_size("wa")
    owners = planes * lax.axis_size("facet")
    cap = max(2, (2 * sub_count + owners - 1) // owners)
    slots = owners * cap
    sent = pack(
        routes.reshape(sub_count),
        offsets.reshape(2 * sub_count),
        uv_angles.reshape(sub_count, 2 * count_vis),
        visibilities.reshape(sub_count, 2 * count_vis).astype(jnp.float32),
        owners,
        cap,
    )
    got = lax.all_to_all(sent, ("wa", "facet"), split_axis=0, concat_axis=0, tiled=True)
    got = got.reshape(owners, 3, cap, LANES)
    first, second = dft_tables(grid_n)
    image = form_image(
        got[:, 2, :, 0:2].astype(jnp.int32).reshape(2 * slots),
        got[:, 0].reshape(slots, LANES),
        got[:, 1].reshape(slots, LANES),
        jnp.asarray(first),
        jnp.asarray(second),
        grid_n,
    )
    phase_re = jnp.cos(pixel_phase[0])
    phase_im = jnp.sin(pixel_phase[0])
    plane = lax.axis_index("wa")
    rows = grid_n // CHUNKS
    outs = []
    for c in range(CHUNKS):
        part = slice(c * rows, (c + 1) * rows)
        own = image[part]
        running = own
        for hop in range(1, planes):
            incoming = lax.ppermute(
                running.astype(jnp.bfloat16), "wa", [(hop - 1, hop)]
            ).astype(jnp.float32)
            re, im = incoming[:, :grid_n], incoming[:, grid_n:]
            turned = jnp.concatenate(
                [
                    phase_re[part] * re - phase_im[part] * im,
                    phase_re[part] * im + phase_im[part] * re,
                ],
                axis=1,
            )
            running = jnp.where(plane == hop, turned + own, running)
        outs.append(running)
    return jnp.concatenate(outs, axis=0).reshape(1, 1, grid_n, 2 * grid_n)


def solution(mesh):
    in_specs = (
        P(("wa", "facet"), None, None),
        P(("wa", "facet"), None, None),
        P(("wa", "facet"), None),
        P(("wa", "facet"), None),
        P("facet", None, None),
    )
    out_specs = P("wa", "facet", None, None)
    return jax.shard_map(
        on_device, mesh=mesh, in_specs=in_specs, out_specs=out_specs, check_vma=False
    )
```

time: 572 us -> 127 us (0.22)
  other arithmetic: 276 us -> 17.4 us
  matrix products: 110 us -> 0 us
  waiting for transfers between devices: 138 us -> 56.9 us
  Pallas kernels: 0 us -> 23.2 us
  local copies, waits for them, and re-layouts: 22.2 us -> 9.49 us
    scatter-add x16 -> x0, other arithmetic: 177 us -> none  [add_piece(): running_grid.at[row_targets].add(placed.reshape(-1, 2 * grid_n))]
    dot_general x50 -> x0, matrix products: 110 us -> none  [the longest x16 75.1 us: add_piece(): jnp.einsum('bcd,bdj->bcj', piece_data, place_table, preferred_element_typ...]
    ppermute x3 -> x12, waiting for transfers between devices: 138 us -> 46.8 us  [on_device(): lax.ppermute(running.astype(jnp.bfloat16), 'wa', [(hop - 1, hop)])]
    another operation x36 -> x0, other arithmetic: 77.9 us -> none
    pallas_call x0 -> x2, Pallas kernels: none -> 23.2 us  [the longest x1 20.6 us: form_image(): pl.pallas_call(functools.partial(image_kernel, grid_n), out_shape=jax.Sha...]
    all_to_all x3 -> x1, starting transfers between devices: 17.5 us -> 5.86 us  [on_device(): lax.all_to_all(sent, ('wa', 'facet'), split_axis=0, concat_axis=0, tiled=...]
    convert_element_type x33 -> x17, other arithmetic: 0.9 us -> 11 us  [the longest x12 6.3 us: on_device(): incoming = lax.ppermute(running.astype(jnp.bfloat16), 'wa', [(hop - 1, ho...]
    all_to_all x3 -> x1, waiting for transfers between devices: 0.01 us -> 10 us  [on_device(): lax.all_to_all(sent, ('wa', 'facet'), split_axis=0, concat_axis=0, tiled=...]
  transfers between devices with their start and end apart: 6 -> 13, of which waited for: 3 -> 5; matrix products, arithmetic and copies ran while one was open for 4% -> 12% of each run, Pallas kernels for 0% -> 0%
where the time goes in v1:
time: 127 us; the launch traced here: 126 us
  waiting for transfers between devices  56.9 us (45%)
  Pallas kernels  23.2 us (18%)
  starting transfers between devices  18.7 us (15%)
  other arithmetic  17.4 us (14%)
  local copies, waits for them, and re-layouts  9.49 us (7%)
    ppermute x12, waiting for transfers between devices, on_device(): lax.ppermute(running.astype(jnp.bfloat16), 'wa', [(hop - 1, hop)])  46.8 us
    pallas_call x1, Pallas kernels, form_image(): pl.pallas_call(functools.partial(image_kernel, grid_n), out_shape=jax.Sha...  20.6 us
    ppermute x12, starting transfers between devices, on_device(): lax.ppermute(running.astype(jnp.bfloat16), 'wa', [(hop - 1, hop)])  12.8 us
    all_to_all x1, waiting for transfers between devices, on_device(): lax.all_to_all(sent, ('wa', 'facet'), split_axis=0, concat_axis=0, tiled=...  10 us
    convert_element_type x12, other arithmetic, on_device(): incoming = lax.ppermute(running.astype(jnp.bfloat16), 'wa', [(hop - 1, ho...  6.3 us
    all_to_all x1, starting transfers between devices, on_device(): lax.all_to_all(sent, ('wa', 'facet'), split_axis=0, concat_axis=0, tiled=...  5.86 us
    sub x7, other arithmetic, on_device(): phase_re[part] * re - phase_im[part] * im  4.06 us
    convert_element_type x3, other arithmetic, on_device(): running.astype(jnp.bfloat16)  3.89 us
  transfers between devices with their start and end apart: 13, of which 5 were waited for; matrix products, arithmetic and copies ran while one was open for 12% of the time, Pallas kernels for 0%

profile of v1, /device:TPU:26, one launch (start us, length us, event | category | flops | bytes accessed | tf_op | source)
XLA Modules:
  0.0 126.4 jit_solution(3882993218134652630)
XLA Ops:
  0.0 0.9 bitcast_convert_fusion
  1.6 1.6 %copy.11.angles = f32[128,128]{1,0:T(8,128)} copy(f32[128,128]{0,1:T(8,128)} %bitcast.130) | data formatting | bytes 131072 | tf_op jit(solution)/shard_map/reshape | solution.py:273
  4.7 2.6 %pack.1 = f32[768,128]{1,0:T(8,128)} custom-call(s32[128]{0:T(128)} %bitcast.131, s32[256]{0:T(256)} %reshape.35.offsets, f32[128,128]{1,0:T(8,128)} %copy.11.angles, f32[128,128]{1,0:T(8,128)} %copy.12.vis), custom_call_target="tpu_custom_call" | custom-call | tf_op jit(solution)/shard_map/pack/pallas_call | solution.py:71
  7.2 5.9 %all-to-all-start = ((f32[32,24,128]{2,1,0:T(8,128)}), f32[32,24,128]{2,1,0:T(8,128)S(1)}, u32[]{:S(2)}, u32[]{:S(2)}) async-start(f32[32,24,128]{2,1,0:T(8,128)} %bitcast.129), calls=%async_computation | async-start | bytes 786432 | tf_op jit(solution)/shard_map/all_to_all | solution.py:278
  13.1 10.0 %all-to-all-done = f32[32,24,128]{2,1,0:T(8,128)S(1)} async-done(((f32[32,24,128]{2,1,0:T(8,128)}), f32[32,24,128]{2,1,0:T(8,128)S(1)}, u32[]{:S(2)}, u32[]{:S(2)}) %all-to-all-start) | async-done | bytes 393248 | tf_op jit(solution)/shard_map/all_to_all | solution.py:278
  23.3 1.6 %copy-done = bf16[1024,1024]{1,0:T(8,128)(2,1)S(1)} copy-done((bf16[1024,1024]{1,0:T(8,128)(2,1)S(1)}, bf16[1024,1024]{1,0:T(8,128)(2,1)}, u32[]{:S(2)}) %copy-start) | copy-done | bytes 2097176
  24.9 20.6 %image.1 = f32[512,1024]{1,0:T(8,128)S(1)} custom-call(s32[512]{0:T(512)S(1)} %convert_element_type.87.offsets, f32[256,128]{1,0:T(8,128)S(1)} %get-tuple-element.66.angles, f32[256,128]{1,0:T(8,128)S(1)} %get-tuple-element.65.vis, bf16[512,1024]{1,0:T(8,128)(2,1)S(1)} %copy-done.1, bf16[1024,1024]{1,0:T(8,128)(2,1)S(1)} %copy-done), custom_call_target="tpu_custom_call" | custom-call | tf_op jit(solution)/shard_map/image/pallas_call | solution.py:231
  47.9 3.7 %fusion.21 = (f32[1,512,512]{2,1,0:T(8,128)S(1)}, f32[1,512,512]{2,1,0:T(8,128)S(1)}) fusion(f32[1,512,512]{2,1,0:T(8,128)S(1)} %copy-done.23), kind=kLoop, calls=%fused_computation.70 | loop fusion | bytes 3145728 | tf_op jit(solution)/shard_map/sin | solution.py:290
  53.1 1.3 %fusion.8 = (bf16[128,1024]{1,0:T(8,128)(2,1)}, bf16[128,1024]{1,0:T(8,128)(2,1)}, bf16[128,1024]{1,0:T(8,128)(2,1)}, bf16[128,1024]{1,0:T(8,128)(2,1)}) fusion(f32[512,1024]{1,0:T(8,128)S(1)} %image.1, f32[128,512]{1,0:T(8,128)S(1)} %get-tuple-element.18, f32[128,512]{1,0:T(8,128)S(1)} %get-tuple-element.17, pred[]{:T(512)S(6)} %eq.8, ...), kind=kLoop, calls=%fused_computation.60 | loop fusion | flops 2097152 | bytes 5242881 | tf_op jit(solution)/shard_map/convert_element_type | solution.py:300
  54.5 1.4 %collective-permute-start.1 = (bf16[128,1024]{1,0:T(8,128)(2,1)}, bf16[128,1024]{1,0:T(8,128)(2,1)}, u32[]{:S(2)}, u32[]{:S(2)}) collective-permute-start(bf16[128,1024]{1,0:T(8,128)(2,1)} %get-tuple-element.49), channel_id=1, source_target_pairs={{8,16},{9,17},{10,18},{11,19},{12,20},{13,21},{14,22},{15,23}} | collective-permute-start | bytes 786440 | tf_op jit(solution)/shard_map/ppermute | solution.py:299
  55.9 1.4 %collective-permute-start.4 = (bf16[128,1024]{1,0:T(8,128)(2,1)}, bf16[128,1024]{1,0:T(8,128)(2,1)}, u32[]{:S(2)}, u32[]{:S(2)}) collective-permute-start(bf16[128,1024]{1,0:T(8,128)(2,1)} %get-tuple-element.50), channel_id=1, source_target_pairs={{8,16},{9,17},{10,18},{11,19},{12,20},{13,21},{14,22},{15,23}} | collective-permute-start | bytes 786440 | tf_op jit(solution)/shard_map/ppermute | solution.py:299
  57.2 1.3 %collective-permute-start.7 = (bf16[128,1024]{1,0:T(8,128)(2,1)}, bf16[128,1024]{1,0:T(8,128)(2,1)}, u32[]{:S(2)}, u32[]{:S(2)}) collective-permute-start(bf16[128,1024]{1,0:T(8,128)(2,1)} %get-tuple-element.51), channel_id=1, source_target_pairs={{8,16},{9,17},{10,18},{11,19},{12,20},{13,21},{14,22},{15,23}} | collective-permute-start | bytes 786440 | tf_op jit(solution)/shard_map/ppermute | solution.py:299
  59.4 1.0 convert_element_type.91
  60.4 1.0 convert_element_type.97
  61.4 1.1 multiply_subtract_fusion.7
  62.5 1.1 convert_element_type.103
  63.9 1.5 %fusion.12 = (bf16[128,1024]{1,0:T(8,128)(2,1)S(1)}, f32[128,1024]{1,0:T(8,128)}, bf16[128,1024]{1,0:T(8,128)(2,1)}, f32[128,1024]{1,0:T(8,128)}, bf16[128,1024]{1,0:T(8,128)(2,1)}, /*index=5*/f32[128,1024]{1,0:T(8,128)}) fusion(f32[128,512]{1,0:T(8,128)S(1)} %copy-done.18, f32[128,512]{1,0:T(8,128)S(1)} %copy-done.16, pred[]{:T(512)S(6)} %eq.8, ...), kind=kLoop, calls=%fused_computation.65 | loop fusion | flops 2752512 | bytes 7077890 | tf_op jit(solution)/shard_map/convert_element_type | solution.py:300
  65.5 1.3 %collective-permute-start.2 = (bf16[128,1024]{1,0:T(8,128)(2,1)S(1)}, bf16[128,1024]{1,0:T(8,128)(2,1)S(1)}, u32[]{:S(2)}, u32[]{:S(2)}) collective-permute-start(bf16[128,1024]{1,0:T(8,128)(2,1)S(1)} %get-tuple-element.5), channel_id=1, source_target_pairs={{16,24},{17,25},{18,26},{19,27},{20,28},{21,29},{22,30},{23,31}} | collective-permute-start | bytes 786440 | tf_op jit(solution)/shard_map/ppermute | solution.py:299
  66.7 1.3 %collective-permute-start.8 = (bf16[128,1024]{1,0:T(8,128)(2,1)}, bf16[128,1024]{1,0:T(8,128)(2,1)}, u32[]{:S(2)}, u32[]{:S(2)}) collective-permute-start(bf16[128,1024]{1,0:T(8,128)(2,1)} %get-tuple-element.43), channel_id=1, source_target_pairs={{16,24},{17,25},{18,26},{19,27},{20,28},{21,29},{22,30},{23,31}} | collective-permute-start | bytes 786440 | tf_op jit(solution)/shard_map/ppermute | solution.py:299
  68.0 1.3 %collective-permute-start.5 = (bf16[128,1024]{1,0:T(8,128)(2,1)}, bf16[128,1024]{1,0:T(8,128)(2,1)}, u32[]{:S(2)}, u32[]{:S(2)}) collective-permute-start(bf16[128,1024]{1,0:T(8,128)(2,1)} %get-tuple-element.45), channel_id=1, source_target_pairs={{16,24},{17,25},{18,26},{19,27},{20,28},{21,29},{22,30},{23,31}} | collective-permute-start | bytes 786440 | tf_op jit(solution)/shard_map/ppermute | solution.py:299
  69.4 39.1 %collective-permute-done.2 = bf16[128,1024]{1,0:T(8,128)(2,1)S(1)} collective-permute-done((bf16[128,1024]{1,0:T(8,128)(2,1)S(1)}, bf16[128,1024]{1,0:T(8,128)(2,1)S(1)}, u32[]{:S(2)}, u32[]{:S(2)}) %collective-permute-start.2) | collective-permute-done | bytes 262176 | tf_op jit(solution)/shard_map/ppermute | solution.py:299
  108.5 1.0 multiply_subtract_fusion.9
  109.5 1.0 fusion.18
  110.6 1.3 %collective-permute-start.11 = (bf16[128,1024]{1,0:T(8,128)(2,1)}, bf16[128,1024]{1,0:T(8,128)(2,1)}, u32[]{:S(2)}, u32[]{:S(2)}) collective-permute-start(bf16[128,1024]{1,0:T(8,128)(2,1)} %get-tuple-element.11), channel_id=1, source_target_pairs={{16,24},{17,25},{18,26},{19,27},{20,28},{21,29},{22,30},{23,31}} | collective-permute-start | bytes 786440 | tf_op jit(solution)/shard_map/ppermute | solution.py:299
  111.9 2.3 %collective-permute-done.8 = bf16[128,1024]{1,0:T(8,128)(2,1)} collective-permute-done((bf16[128,1024]{1,0:T(8,128)(2,1)}, bf16[128,1024]{1,0:T(8,128)(2,1)}, u32[]{:S(2)}, u32[]{:S(2)}) %collective-permute-start.8) | collective-permute-done | bytes 262176 | tf_op jit(solution)/shard_map/ppermute | solution.py:299
  114.2 1.0 convert_element_type.105
  115.2 4.6 %collective-permute-done.5 = bf16[128,1024]{1,0:T(8,128)(2,1)} collective-permute-done((bf16[128,1024]{1,0:T(8,128)(2,1)}, bf16[128,1024]{1,0:T(8,128)(2,1)}, u32[]{:S(2)}, u32[]{:S(2)}) %collective-permute-start.5) | collective-permute-done | bytes 262176 | tf_op jit(solution)/shard_map/ppermute | solution.py:299
  119.8 1.0 convert_element_type.99
  120.8 1.1 multiply_subtract_fusion.3
  121.9 0.8 collective-permute-done.11
  122.7 1.0 convert_element_type.111
  124.8 1.6 %maximum_bitcast_fusion = f32[1,1,512,1024]{3,2,1,0:T(8,128)} fusion(f32[128,1024]{1,0:T(8,128)S(1)} %get-tuple-element.40, f32[128,1024]{1,0:T(8,128)S(1)} %get-tuple-element.39, f32[128,1024]{1,0:T(8,128)S(1)} %get-tuple-element.38, f32[128,1024]{1,0:T(8,128)S(1)} %get-tuple-element.37), kind=kLoop, calls=%fused_computation | loop fusion | flops 1572864 | bytes 4194304 | tf_op jit(solution)/shard_map/reshape | solution.py:312
  (82 shorter events, 8.3 us)
Async XLA Ops:
  0.0 23.3 %copy-start.1 = (bf16[512,1024]{1,0:T(8,128)(2,1)S(1)}, bf16[512,1024]{1,0:T(8,128)(2,1)}, u32[]{:S(2)}) copy-start(bf16[512,1024]{1,0:T(8,128)(2,1)} %constant.15.clone.first_hbm) | copy-start | bytes 3145732
  7.2 15.9 %all-to-all-start = ((f32[32,24,128]{2,1,0:T(8,128)}), f32[32,24,128]{2,1,0:T(8,128)S(1)}, u32[]{:S(2)}, u32[]{:S(2)}) async-start(f32[32,24,128]{2,1,0:T(8,128)} %bitcast.129), calls=%async_computation | async-start | bytes 786432 | tf_op jit(solution)/shard_map/all_to_all | solution.py:278
  23.3 1.6 %copy-start = (bf16[1024,1024]{1,0:T(8,128)(2,1)S(1)}, bf16[1024,1024]{1,0:T(8,128)(2,1)}, u32[]{:S(2)}) copy-start(bf16[1024,1024]{1,0:T(8,128)(2,1)} %constant.16.clone.second_hbm) | copy-start | bytes 6291460
  45.5 2.4 %copy-start.23 = (f32[1,512,512]{2,1,0:T(8,128)S(1)}, f32[1,512,512]{2,1,0:T(8,128)}, u32[]{:S(2)}) copy-start(f32[1,512,512]{2,1,0:T(8,128)} %param.11) | copy-start | bytes 3145732
  45.7 6.6 %collective-permute-start = (bf16[128,1024]{1,0:T(8,128)(2,1)S(1)}, bf16[128,1024]{1,0:T(8,128)(2,1)S(1)}, u32[]{:S(2)}, u32[]{:S(2)}) collective-permute-start(bf16[128,1024]{1,0:T(8,128)(2,1)S(1)} %get-tuple-element.55), channel_id=1, source_target_pairs={{0,8},{1,9},{2,10},{3,11},{4,12},{5,13},{6,14},{7,15}} | collective-permute-start | bytes 786440 | tf_op jit(solution)/shard_map/ppermute | solution.py:299
  46.5 5.8 %collective-permute-start.6 = (bf16[128,1024]{1,0:T(8,128)(2,1)S(1)}, bf16[128,1024]{1,0:T(8,128)(2,1)S(1)}, u32[]{:S(2)}, u32[]{:S(2)}) collective-permute-start(bf16[128,1024]{1,0:T(8,128)(2,1)S(1)} %get-tuple-element.57), channel_id=1, source_target_pairs={{0,8},{1,9},{2,10},{3,11},{4,12},{5,13},{6,14},{7,15}} | collective-permute-start | bytes 786440 | tf_op jit(solution)/shard_map/ppermute | solution.py:299
  47.2 5.2 %collective-permute-start.3 = (bf16[128,1024]{1,0:T(8,128)(2,1)S(1)}, bf16[128,1024]{1,0:T(8,128)(2,1)S(1)}, u32[]{:S(2)}, u32[]{:S(2)}) collective-permute-start(bf16[128,1024]{1,0:T(8,128)(2,1)S(1)} %get-tuple-element.58), channel_id=1, source_target_pairs={{0,8},{1,9},{2,10},{3,11},{4,12},{5,13},{6,14},{7,15}} | collective-permute-start | bytes 786440 | tf_op jit(solution)/shard_map/ppermute | solution.py:299
  51.6 1.1 collective-permute-start.9
  52.7 1.7 %copy-start.7 = (f32[128,512]{1,0:T(8,128)}, f32[128,512]{1,0:T(8,128)S(1)}, u32[]{:S(2)}) copy-start(f32[128,512]{1,0:T(8,128)S(1)} %get-tuple-element.23) | copy-start | bytes 786436
  52.7 1.7 %copy-start.9 = (f32[128,512]{1,0:T(8,128)}, f32[128,512]{1,0:T(8,128)S(1)}, u32[]{:S(2)}) copy-start(f32[128,512]{1,0:T(8,128)S(1)} %get-tuple-element.24) | copy-start | bytes 786436
  52.7 1.7 %copy-start.11 = (f32[128,512]{1,0:T(8,128)}, f32[128,512]{1,0:T(8,128)S(1)}, u32[]{:S(2)}) copy-start(f32[128,512]{1,0:T(8,128)S(1)} %get-tuple-element.61) | copy-start | bytes 786436
  52.7 1.7 %copy-start.13 = (f32[128,512]{1,0:T(8,128)}, f32[128,512]{1,0:T(8,128)S(1)}, u32[]{:S(2)}) copy-start(f32[128,512]{1,0:T(8,128)S(1)} %get-tuple-element.62) | copy-start | bytes 786436
  54.5 4.9 %collective-permute-start.1 = (bf16[128,1024]{1,0:T(8,128)(2,1)}, bf16[128,1024]{1,0:T(8,128)(2,1)}, u32[]{:S(2)}, u32[]{:S(2)}) collective-permute-start(bf16[128,1024]{1,0:T(8,128)(2,1)} %get-tuple-element.49), channel_id=1, source_target_pairs={{8,16},{9,17},{10,18},{11,19},{12,20},{13,21},{14,22},{15,23}} | collective-permute-start | bytes 786440 | tf_op jit(solution)/shard_map/ppermute | solution.py:299
  55.9 4.5 %collective-permute-start.4 = (bf16[128,1024]{1,0:T(8,128)(2,1)}, bf16[128,1024]{1,0:T(8,128)(2,1)}, u32[]{:S(2)}, u32[]{:S(2)}) collective-permute-start(bf16[128,1024]{1,0:T(8,128)(2,1)} %get-tuple-element.50), channel_id=1, source_target_pairs={{8,16},{9,17},{10,18},{11,19},{12,20},{13,21},{14,22},{15,23}} | collective-permute-start | bytes 786440 | tf_op jit(solution)/shard_map/ppermute | solution.py:299
  57.2 5.3 %collective-permute-start.7 = (bf16[128,1024]{1,0:T(8,128)(2,1)}, bf16[128,1024]{1,0:T(8,128)(2,1)}, u32[]{:S(2)}, u32[]{:S(2)}) collective-permute-start(bf16[128,1024]{1,0:T(8,128)(2,1)} %get-tuple-element.51), channel_id=1, source_target_pairs={{8,16},{9,17},{10,18},{11,19},{12,20},{13,21},{14,22},{15,23}} | collective-permute-start | bytes 786440 | tf_op jit(solution)/shard_map/ppermute | solution.py:299
  58.6 5.1 %copy-start.3 = (f32[1,512,512]{2,1,0:T(8,128)S(1)}, f32[1,512,512]{2,1,0:T(8,128)}, u32[]{:S(2)}) copy-start(f32[1,512,512]{2,1,0:T(8,128)} %copy-done.2) | copy-start | bytes 3145732
  58.6 10.8 %collective-permute-start.10 = (bf16[128,1024]{1,0:T(8,128)(2,1)}, bf16[128,1024]{1,0:T(8,128)(2,1)S(1)}, u32[]{:S(2)}, u32[]{:S(2)}) collective-permute-start(bf16[128,1024]{1,0:T(8,128)(2,1)} %get-tuple-element.52), channel_id=1, source_target_pairs={{8,16},{9,17},{10,18},{11,19},{12,20},{13,21},{14,22},{15,23}} | collective-permute-start | bytes 786440 | tf_op jit(solution)/shard_map/ppermute | solution.py:299
  62.4 1.4 %copy-start.8 = (f32[128,512]{1,0:T(8,128)S(1)}, f32[128,512]{1,0:T(8,128)}, u32[]{:S(2)}) copy-start(f32[128,512]{1,0:T(8,128)} %copy-done.7) | copy-start | bytes 786436
  62.5 1.4 %copy-start.10 = (f32[128,512]{1,0:T(8,128)S(1)}, f32[128,512]{1,0:T(8,128)}, u32[]{:S(2)}) copy-start(f32[128,512]{1,0:T(8,128)} %copy-done.9) | copy-start | bytes 786436
  62.5 1.4 %copy-start.12 = (f32[128,512]{1,0:T(8,128)S(1)}, f32[128,512]{1,0:T(8,128)}, u32[]{:S(2)}) copy-start(f32[128,512]{1,0:T(8,128)} %copy-done.11) | copy-start | bytes 786436
  65.5 43.0 %collective-permute-start.2 = (bf16[128,1024]{1,0:T(8,128)(2,1)S(1)}, bf16[128,1024]{1,0:T(8,128)(2,1)S(1)}, u32[]{:S(2)}, u32[]{:S(2)}) collective-permute-start(bf16[128,1024]{1,0:T(8,128)(2,1)S(1)} %get-tuple-element.5), channel_id=1, source_target_pairs={{16,24},{17,25},{18,26},{19,27},{20,28},{21,29},{22,30},{23,31}} | collective-permute-start | bytes 786440 | tf_op jit(solution)/shard_map/ppermute | solution.py:299
  66.7 47.5 %collective-permute-start.8 = (bf16[128,1024]{1,0:T(8,128)(2,1)}, bf16[128,1024]{1,0:T(8,128)(2,1)}, u32[]{:S(2)}, u32[]{:S(2)}) collective-permute-start(bf16[128,1024]{1,0:T(8,128)(2,1)} %get-tuple-element.43), channel_id=1, source_target_pairs={{16,24},{17,25},{18,26},{19,27},{20,28},{21,29},{22,30},{23,31}} | collective-permute-start | bytes 786440 | tf_op jit(solution)/shard_map/ppermute | solution.py:299
  68.0 51.8 %collective-permute-start.5 = (bf16[128,1024]{1,0:T(8,128)(2,1)}, bf16[128,1024]{1,0:T(8,128)(2,1)}, u32[]{:S(2)}, u32[]{:S(2)}) collective-permute-start(bf16[128,1024]{1,0:T(8,128)(2,1)} %get-tuple-element.45), channel_id=1, source_target_pairs={{16,24},{17,25},{18,26},{19,27},{20,28},{21,29},{22,30},{23,31}} | collective-permute-start | bytes 786440 | tf_op jit(solution)/shard_map/ppermute | solution.py:299
  69.4 40.1 %copy-start.6 = (f32[128,512]{1,0:T(8,128)S(1)}, f32[128,512]{1,0:T(8,128)}, u32[]{:S(2)}) copy-start(f32[128,512]{1,0:T(8,128)} %copy-done.5) | copy-start | bytes 786436
  110.6 12.2 %collective-permute-start.11 = (bf16[128,1024]{1,0:T(8,128)(2,1)}, bf16[128,1024]{1,0:T(8,128)(2,1)}, u32[]{:S(2)}, u32[]{:S(2)}) collective-permute-start(bf16[128,1024]{1,0:T(8,128)(2,1)} %get-tuple-element.11), channel_id=1, source_target_pairs={{16,24},{17,25},{18,26},{19,27},{20,28},{21,29},{22,30},{23,31}} | collective-permute-start | bytes 786440 | tf_op jit(solution)/shard_map/ppermute | solution.py:299
  111.9 11.9 %copy-start.4 = (f32[1,512,512]{2,1,0:T(8,128)S(1)}, f32[1,512,512]{2,1,0:T(8,128)}, u32[]{:S(2)}) copy-start(f32[1,512,512]{2,1,0:T(8,128)} %copy-done.2) | copy-start | bytes 3145732
  121.9 2.1 %copy-start.19 = (f32[128,1024]{1,0:T(8,128)S(1)}, f32[128,1024]{1,0:T(8,128)}, u32[]{:S(2)}) copy-start(f32[128,1024]{1,0:T(8,128)} %get-tuple-element.12) | copy-start | bytes 1572868
  121.9 2.1 %copy-start.20 = (f32[128,1024]{1,0:T(8,128)S(1)}, f32[128,1024]{1,0:T(8,128)}, u32[]{:S(2)}) copy-start(f32[128,1024]{1,0:T(8,128)} %get-tuple-element.6) | copy-start | bytes 1572868
  121.9 2.1 %copy-start.21 = (f32[128,1024]{1,0:T(8,128)S(1)}, f32[128,1024]{1,0:T(8,128)}, u32[]{:S(2)}) copy-start(f32[128,1024]{1,0:T(8,128)} %get-tuple-element.44) | copy-start | bytes 1572868
  121.9 2.1 %copy-start.22 = (f32[128,1024]{1,0:T(8,128)S(1)}, f32[128,1024]{1,0:T(8,128)}, u32[]{:S(2)}) copy-start(f32[128,1024]{1,0:T(8,128)} %get-tuple-element.46) | copy-start | bytes 1572868
  121.9 2.1 %copy-start.24 = (f32[128,512]{1,0:T(8,128)S(1)}, f32[128,512]{1,0:T(8,128)}, u32[]{:S(2)}) copy-start(f32[128,512]{1,0:T(8,128)} %get-tuple-element.13) | copy-start | bytes 786436
  121.9 2.1 %copy-start.25 = (f32[128,512]{1,0:T(8,128)S(1)}, f32[128,512]{1,0:T(8,128)}, u32[]{:S(2)}) copy-start(f32[128,512]{1,0:T(8,128)} %get-tuple-element.14) | copy-start | bytes 786436
  (7 other events, 9.7 us)

commit v2 on v1

--- a/solution.py
+++ b/solution.py
@@ -13,7 +13,7 @@
 LANES = 128
 ROWS = 8
 GROUP = 8
-CHUNKS = 4
+PARTS = (7, 7, 7, 6, 5)
 SINE = tuple(
     float(v)
     for v in np.linalg.lstsq(
@@ -40,8 +40,10 @@
     return total * x
 
 
-def pack_kernel(owners, cap, routes, offsets, angles, vis, out, counts):
+def pack_kernel(owners, cap, routes, offsets, angles, vis, out, counts, angle_rows, vis_rows):
     out[...] = jnp.zeros_like(out)
+    angle_rows[...] = angles[...].T
+    vis_rows[...] = vis[...].astype(jnp.float32).T
 
     def clear(i, _):
         counts[i] = 0
@@ -51,18 +53,18 @@
     lane = lax.broadcasted_iota(jnp.int32, (1, LANES), 1)
 
     def place(i, _):
-        owner = routes[i]
+        owner = routes[0, i]
         rank = counts[owner]
         counts[owner] = rank + 1
         base = owner * (3 * cap) + rank
-        out[pl.ds(base, 1), :] = angles[pl.ds(i, 1), :]
-        out[pl.ds(base + cap, 1), :] = vis[pl.ds(i, 1), :]
-        first, second = offsets[2 * i], offsets[2 * i + 1]
+        out[pl.ds(base, 1), :] = angle_rows[pl.ds(i, 1), :]
+        out[pl.ds(base + cap, 1), :] = vis_rows[pl.ds(i, 1), :]
+        first, second = offsets[0, i], offsets[1, i]
         meta = jnp.where(lane == 0, first, jnp.where(lane == 1, second, 0))
         out[pl.ds(base + 2 * cap, 1), :] = meta.astype(jnp.float32)
         return 0
 
-    lax.fori_loop(0, angles.shape[0], place, 0, unroll=4)
+    lax.fori_loop(0, angles.shape[1], place, 0, unroll=4)
 
 
 def pack(routes, offsets, angles, vis, owners, cap):
@@ -73,12 +75,25 @@
         out_shape=jax.ShapeDtypeStruct((owners * cap * 3, LANES), jnp.float32),
         in_specs=[smem, smem, vmem, vmem],
         out_specs=vmem,
-        scratch_shapes=[pltpu.SMEM((owners,), jnp.int32)],
+        scratch_shapes=[
+            pltpu.SMEM((owners,), jnp.int32),
+            pltpu.VMEM(angles.shape[::-1], jnp.float32),
+            pltpu.VMEM(vis.shape[::-1], jnp.float32),
+        ],
         name="pack",
     )(routes, offsets, angles, vis)
 
 
 def image_kernel(
+    grid_n, bounds, offsets, angles, vis, first_hbm, second_hbm, out, *rest
+):
+    sends = rest[: len(bounds) - 1]
+    image_body(grid_n, offsets, angles, vis, first_hbm, second_hbm, out, *rest[len(bounds) - 1 :])
+    for i, send in enumerate(sends):
+        send[...] = out[bounds[i] : bounds[i + 1], :].astype(jnp.bfloat16)
+
+
+def image_body(
     grid_n, offsets, angles, vis, first_hbm, second_hbm, out,
     tables, turns_u, turns_v, amp_a, amp_b, grid, dense, first, second, sems,
 ):
@@ -221,18 +236,19 @@
     lax.fori_loop(0, grid_n // step, transform, 0)
 
 
-def form_image(offsets, angles, vis, first, second, grid_n):
+def form_image(offsets, angles, vis, first, second, grid_n, bounds):
     slots = angles.shape[0]
     blocks = grid_n // SUB
     smem = pl.BlockSpec(memory_space=pltpu.SMEM)
     vmem = pl.BlockSpec(memory_space=pltpu.VMEM)
-    anywhere = pl.BlockSpec(memory_space=pl.ANY)
+    hbm = pl.BlockSpec(memory_space=pltpu.HBM)
     line = pltpu.VMEM((slots, LANES), jnp.float32)
     return pl.pallas_call(
-        functools.partial(image_kernel, grid_n),
-        out_shape=jax.ShapeDtypeStruct((grid_n, 2 * grid_n), jnp.float32),
-        in_specs=[smem, vmem, vmem, anywhere, anywhere],
-        out_specs=vmem,
+        functools.partial(image_kernel, grid_n, bounds),
+        out_shape=[pltpu.VMEM((grid_n, 2 * grid_n), jnp.float32)]
+        + [pltpu.VMEM((b - a, 2 * grid_n), jnp.bfloat16) for a, b in zip(bounds, bounds[1:])],
+        in_specs=[smem, vmem, vmem, hbm, hbm],
+        out_specs=[vmem] * len(bounds),
         scratch_shapes=[
             pltpu.VMEM((slots, 8, ROWS, LANES), jnp.float32),
             line, line, line, line,
@@ -242,7 +258,7 @@
             pltpu.VMEM(second.shape, jnp.bfloat16),
             pltpu.SemaphoreType.DMA((2,)),
         ],
-        compiler_params=pltpu.CompilerParams(vmem_limit_bytes=40 * 1024 * 1024),
+        compiler_params=pltpu.CompilerParams(vmem_limit_bytes=32 * 1024 * 1024),
         name="image",
     )(offsets, angles, vis, first, second)
 
@@ -259,6 +275,72 @@
     return first.astype(np.float32).astype(jnp.bfloat16), second.astype(np.float32).astype(jnp.bfloat16)
 
 
+def phase_kernel(phase, turns):
+    grid_n = phase.shape[1]
+    step = math.gcd(grid_n, LANES)
+
+    def some(i, _):
+        rows = pl.ds(pl.multiple_of(i * step, step), step)
+        part = phase[rows, :] * (1.0 / (2.0 * math.pi))
+        turns[rows, :grid_n] = sine_turns(part + 0.25)
+        turns[rows, grid_n:] = sine_turns(part)
+        return 0
+
+    lax.fori_loop(0, grid_n // step, some, 0)
+
+
+def phase_tables(phase):
+    grid_n = phase.shape[1]
+    vmem = pl.BlockSpec(memory_space=pltpu.VMEM)
+    return pl.pallas_call(
+        phase_kernel,
+        out_shape=pltpu.VMEM((grid_n, 2 * grid_n), jnp.float32),
+        in_specs=[vmem],
+        out_specs=vmem,
+        compiler_params=pltpu.CompilerParams(vmem_limit_bytes=8 * 1024 * 1024),
+        name="phases",
+    )(phase)
+
+
+def send_up(part, hop):
+    return lax.ppermute(part, "wa", [(hop - 1, hop)])
+
+
+def horner_kernel(hop, start, incoming, image, turns, *outs):
+    grid_n = image.shape[1] // 2
+    rows = pl.ds(start, incoming.shape[0])
+    re_cells, im_cells = pl.ds(0, grid_n), pl.ds(grid_n, grid_n)
+
+    @pl.when(lax.axis_index("wa") == hop)
+    def _():
+        re = incoming[:, re_cells].astype(jnp.float32)
+        im = incoming[:, im_cells].astype(jnp.float32)
+        turn_re, turn_im = turns[rows, re_cells], turns[rows, im_cells]
+        new_re = turn_re * re - turn_im * im + image[rows, re_cells]
+        new_im = turn_re * im + turn_im * re + image[rows, im_cells]
+        outs[-1][rows, re_cells] = new_re
+        outs[-1][rows, im_cells] = new_im
+        for send in outs[:-1]:
+            send[:, re_cells] = new_re.astype(jnp.bfloat16)
+            send[:, im_cells] = new_im.astype(jnp.bfloat16)
+
+
+def horner_step(hop, planes, start, end, incoming, image, turns):
+    vmem = pl.BlockSpec(memory_space=pltpu.VMEM)
+    outs = [pltpu.VMEM((end - start, image.shape[1]), jnp.bfloat16)] * (hop + 1 < planes)
+    outs.append(pltpu.VMEM(image.shape, jnp.float32))
+    got = pl.pallas_call(
+        functools.partial(horner_kernel, hop, start),
+        out_shape=outs,
+        in_specs=[vmem] * 3,
+        out_specs=[vmem] * len(outs),
+        input_output_aliases={1: len(outs) - 1},
+        compiler_params=pltpu.CompilerParams(vmem_limit_bytes=4 * 1024 * 1024),
+        name="horner",
+    )(*(pltpu.with_memory_space_constraint(x, pltpu.VMEM) for x in (incoming, image, turns)))
+    return got[0], got[-1]
+
+
 def on_device(visibilities, uv_angles, routes, offsets, pixel_phase):
     sub_count = visibilities.shape[0]
     count_vis = visibilities.shape[2]
@@ -268,48 +350,39 @@
     cap = max(2, (2 * sub_count + owners - 1) // owners)
     slots = owners * cap
     sent = pack(
-        routes.reshape(sub_count),
-        offsets.reshape(2 * sub_count),
-        uv_angles.reshape(sub_count, 2 * count_vis),
-        visibilities.reshape(sub_count, 2 * count_vis).astype(jnp.float32),
+        routes.T,
+        offsets.T,
+        uv_angles.transpose(1, 2, 0).reshape(2 * count_vis, sub_count),
+        visibilities.transpose(1, 2, 0).reshape(2 * count_vis, sub_count),
         owners,
         cap,
     )
     got = lax.all_to_all(sent, ("wa", "facet"), split_axis=0, concat_axis=0, tiled=True)
     got = got.reshape(owners, 3, cap, LANES)
     first, second = dft_tables(grid_n)
-    image = form_image(
+    units = grid_n // 16
+    bounds = [0] + [16 * (units * sum(PARTS[: i + 1]) // sum(PARTS)) for i in range(len(PARTS))]
+    image, *sends = form_image(
         got[:, 2, :, 0:2].astype(jnp.int32).reshape(2 * slots),
         got[:, 0].reshape(slots, LANES),
         got[:, 1].reshape(slots, LANES),
         jnp.asarray(first),
         jnp.asarray(second),
         grid_n,
+        bounds,
     )
-    phase_re = jnp.cos(pixel_phase[0])
-    phase_im = jnp.sin(pixel_phase[0])
-    plane = lax.axis_index("wa")
-    rows = grid_n // CHUNKS
-    outs = []
-    for c in range(CHUNKS):
-        part = slice(c * rows, (c + 1) * rows)
-        own = image[part]
-        running = own
+    turns = phase_tables(pixel_phase[0])
+    incoming = {(1, c): send_up(sends[c], 1) for c in range(len(sends))}
+    for beat in range(len(sends) + 2 * planes):
         for hop in range(1, planes):
-            incoming = lax.ppermute(
-                running.astype(jnp.bfloat16), "wa", [(hop - 1, hop)]
-            ).astype(jnp.float32)
-            re, im = incoming[:, :grid_n], incoming[:, grid_n:]
-            turned = jnp.concatenate(
-                [
-                    phase_re[part] * re - phase_im[part] * im,
-                    phase_re[part] * im + phase_im[part] * re,
-                ],
-                axis=1,
-            )
-            running = jnp.where(plane == hop, turned + own, running)
-        outs.append(running)
-    return jnp.concatenate(outs, axis=0).reshape(1, 1, grid_n, 2 * grid_n)
+            c = beat - 2 * (hop - 1)
+            if 0 <= c < len(sends):
+                send, image = horner_step(
+                    hop, planes, bounds[c], bounds[c + 1], incoming[hop, c], image, turns
+                )
+                if hop + 1 < planes:
+                    incoming[hop + 1, c] = send_up(send, hop + 1)
+    return image.reshape(1, 1, grid_n, 2 * grid_n)
 
 
 def solution(mesh):

time: 127 us -> 87.3 us (0.69)
  the two profiles are of different devices: /device:TPU:26 before, /device:TPU:24 now
where the time goes in v2:
time: 87.3 us; the launch traced here: 86.9 us
  waiting for transfers between devices  28 us (32%)
  Pallas kernels  26.1 us (30%)
  blocking collectives  16.5 us (19%)
  starting transfers between devices  13.2 us (15%)
  local copies, waits for them, and re-layouts  2.8 us (3%)
    ppermute x15, waiting for transfers between devices, send_up(): return lax.ppermute(part, 'wa', [(hop - 1, hop)])  28 us
    pallas_call x1, Pallas kernels, form_image(): pl.pallas_call(functools.partial(image_kernel, grid_n, bounds), out_shape...  20.8 us
    all_to_all x1, blocking collectives, on_device(): lax.all_to_all(sent, ('wa', 'facet'), split_axis=0, concat_axis=0, tiled=...  16.5 us
    ppermute x15, starting transfers between devices, send_up(): return lax.ppermute(part, 'wa', [(hop - 1, hop)])  13.2 us
    pallas_call x1, Pallas kernels, pack(): pl.pallas_call(functools.partial(pack_kernel, owners, cap), out_shape=jax...  2.85 us
    unnamed x7, local copies, waits for them, and re-layouts  2.65 us
  transfers between devices with their start and end apart: 15, of which 5 were waited for; matrix products, arithmetic and copies ran while one was open for 0% of the time, Pallas kernels for 3%

profile of v2, /device:TPU:24, one launch (start us, length us, event | category | flops | bytes accessed | tf_op | source)
XLA Modules:
  0.0 86.9 jit_solution(15364989267742635383)
XLA Ops:
  0.0 2.8 %pack.1 = f32[768,128]{1,0:T(8,128)} custom-call(s32[1,128]{1,0:T(1,128)} %bitcast.26, s32[2,128]{1,0:T(2,128)} %bitcast.25, f32[128,128]{1,0:T(8,128)} %bitcast.23, bf16[128,128]{1,0:T(8,128)(2,1)} %bitcast.24), custom_call_target="tpu_custom_call" | custom-call | tf_op jit(solution)/shard_map/pack/pallas_call | solution.py:73
  2.9 16.5 %all_to_all.9 = f32[32,24,128]{2,1,0:T(8,128)S(1)} all-to-all(f32[32,24,128]{2,1,0:T(8,128)} %bitcast.22), channel_id=1, replica_groups=mesh['wa'=4,'facet'=8] {'wa','facet'}, dimensions={0} | all-to-all | bytes 786432 | tf_op jit(solution)/shard_map/all_to_all | solution.py:360
  19.4 0.1 convert_element_type.8.offsets
  19.6 1.3 %copy-done.2 = bf16[512,1024]{1,0:T(8,128)(2,1)S(1)} copy-done((bf16[512,1024]{1,0:T(8,128)(2,1)S(1)}, bf16[512,1024]{1,0:T(8,128)(2,1)}, u32[]{:S(2)}) %copy-start.2) | copy-done | bytes 1048600
  20.9 20.8 %image.1 = (f32[512,1024]{1,0:T(8,128)S(1)}, bf16[112,1024]{1,0:T(8,128)(2,1)S(1)}, bf16[112,1024]{1,0:T(8,128)(2,1)S(1)}, bf16[112,1024]{1,0:T(8,128)(2,1)S(1)}...) custom-call(s32[512]{0:T(512)S(1)} %convert_element_type.8.offsets, ...), custom_call_target="tpu_custom_call" | custom-call | tf_op jit(solution)/shard_map/image/pallas_call | solution.py:246
  41.7 0.7 collective-permute-start.2
  42.4 0.7 collective-permute-start.1
  43.0 0.7 collective-permute-start.6
  43.7 1.3 %phases.1.turns = f32[512,1024]{1,0:T(8,128)S(1)} custom-call(f32[512,512]{1,0:T(8,128)S(1)} %bitcast.19), custom_call_target="tpu_custom_call" | custom-call | tf_op jit(solution)/shard_map/phases/pallas_call | solution.py:295
  45.1 0.7 collective-permute-start.5
  45.8 0.7 collective-permute-start.3
  46.5 0.7 collective-permute-start.4
  47.2 0.7 collective-permute-start
  47.9 0.7 collective-permute-start.11
  48.6 1.3 %collective-permute-start.10 = (bf16[112,1024]{1,0:T(8,128)(2,1)S(1)}, bf16[112,1024]{1,0:T(8,128)(2,1)S(1)}, u32[]{:S(2)}, u32[]{:S(2)}) collective-permute-start(bf16[112,1024]{1,0:T(8,128)(2,1)S(1)} %get-tuple-element.48), channel_id=1, source_target_pairs={{16,24},{17,25},{18,26},{19,27},{20,28},{21,29},{22,30},{23,31}} | collective-permute-start | bytes 688136 | tf_op jit(solution)/shard_map/ppermute | solution.py:306
  50.0 1.3 %collective-permute-start.8 = (bf16[112,1024]{1,0:T(8,128)(2,1)S(1)}, bf16[112,1024]{1,0:T(8,128)(2,1)S(1)}, u32[]{:S(2)}, u32[]{:S(2)}) collective-permute-start(bf16[112,1024]{1,0:T(8,128)(2,1)S(1)} %get-tuple-element.46), channel_id=1, source_target_pairs={{16,24},{17,25},{18,26},{19,27},{20,28},{21,29},{22,30},{23,31}} | collective-permute-start | bytes 688136 | tf_op jit(solution)/shard_map/ppermute | solution.py:306
  51.3 0.7 collective-permute-start.9
  52.0 0.7 collective-permute-start.7
  52.7 1.3 %collective-permute-start.14 = (bf16[112,1024]{1,0:T(8,128)(2,1)S(1)}, bf16[112,1024]{1,0:T(8,128)(2,1)S(1)}, u32[]{:S(2)}, u32[]{:S(2)}) collective-permute-start(bf16[112,1024]{1,0:T(8,128)(2,1)S(1)} %get-tuple-element.55), channel_id=1, source_target_pairs={{16,24},{17,25},{18,26},{19,27},{20,28},{21,29},{22,30},{23,31}} | collective-permute-start | bytes 688136 | tf_op jit(solution)/shard_map/ppermute | solution.py:306
  54.0 16.0 %collective-permute-done.10.incoming = bf16[112,1024]{1,0:T(8,128)(2,1)S(1)} collective-permute-done((bf16[112,1024]{1,0:T(8,128)(2,1)S(1)}, bf16[112,1024]{1,0:T(8,128)(2,1)S(1)}, u32[]{:S(2)}, u32[]{:S(2)}) %collective-permute-start.10) | collective-permute-done | bytes 229408 | tf_op jit(solution)/shard_map/ppermute | solution.py:306
  70.0 0.2 horner.23.image
  70.3 1.3 %collective-permute-start.13 = (bf16[96,1024]{1,0:T(8,128)(2,1)S(1)}, bf16[96,1024]{1,0:T(8,128)(2,1)S(1)}, u32[]{:S(2)}, u32[]{:S(2)}) collective-permute-start(bf16[96,1024]{1,0:T(8,128)(2,1)S(1)} %get-tuple-element.54), channel_id=1, source_target_pairs={{16,24},{17,25},{18,26},{19,27},{20,28},{21,29},{22,30},{23,31}} | collective-permute-start | bytes 589832 | tf_op jit(solution)/shard_map/ppermute | solution.py:306
  71.6 3.3 %collective-permute-done.8.incoming = bf16[112,1024]{1,0:T(8,128)(2,1)S(1)} collective-permute-done((bf16[112,1024]{1,0:T(8,128)(2,1)S(1)}, bf16[112,1024]{1,0:T(8,128)(2,1)S(1)}, u32[]{:S(2)}, u32[]{:S(2)}) %collective-permute-start.8) | collective-permute-done | bytes 229408 | tf_op jit(solution)/shard_map/ppermute | solution.py:306
  74.9 0.2 horner.25.image
  75.1 1.3 %collective-permute-start.12 = (bf16[80,1024]{1,0:T(8,128)(2,1)S(1)}, bf16[80,1024]{1,0:T(8,128)(2,1)S(1)}, u32[]{:S(2)}, u32[]{:S(2)}) collective-permute-start(bf16[80,1024]{1,0:T(8,128)(2,1)S(1)} %get-tuple-element.53), channel_id=1, source_target_pairs={{16,24},{17,25},{18,26},{19,27},{20,28},{21,29},{22,30},{23,31}} | collective-permute-start | bytes 491528 | tf_op jit(solution)/shard_map/ppermute | solution.py:306
  76.4 3.4 %collective-permute-done.14.incoming = bf16[112,1024]{1,0:T(8,128)(2,1)S(1)} collective-permute-done((bf16[112,1024]{1,0:T(8,128)(2,1)S(1)}, bf16[112,1024]{1,0:T(8,128)(2,1)S(1)}, u32[]{:S(2)}, u32[]{:S(2)}) %collective-permute-start.14) | collective-permute-done | bytes 229408 | tf_op jit(solution)/shard_map/ppermute | solution.py:306
  79.8 0.2 horner.27.image
  80.0 3.7 %collective-permute-done.13.incoming = bf16[96,1024]{1,0:T(8,128)(2,1)S(1)} collective-permute-done((bf16[96,1024]{1,0:T(8,128)(2,1)S(1)}, bf16[96,1024]{1,0:T(8,128)(2,1)S(1)}, u32[]{:S(2)}, u32[]{:S(2)}) %collective-permute-start.13) | collective-permute-done | bytes 196640 | tf_op jit(solution)/shard_map/ppermute | solution.py:306
  83.7 0.2 horner.28.image
  83.9 1.6 %collective-permute-done.12.incoming = bf16[80,1024]{1,0:T(8,128)(2,1)S(1)} collective-permute-done((bf16[80,1024]{1,0:T(8,128)(2,1)S(1)}, bf16[80,1024]{1,0:T(8,128)(2,1)S(1)}, u32[]{:S(2)}, u32[]{:S(2)}) %collective-permute-start.12) | collective-permute-done | bytes 163872 | tf_op jit(solution)/shard_map/ppermute | solution.py:306
  85.5 0.2 horner.29
  85.6 1.3 %copy.38 = f32[1,1,512,1024]{3,2,1,0:T(8,128)} copy(f32[1,1,512,1024]{3,2,1,0:T(8,128)S(1)} %bitcast.18) | data formatting | bytes 4194304
  (27 shorter events, 0.2 us)
Async XLA Ops:
  0.0 19.6 %copy-start = (bf16[1024,1024]{1,0:T(8,128)(2,1)S(1)}, bf16[1024,1024]{1,0:T(8,128)(2,1)}, u32[]{:S(2)}) copy-start(bf16[1024,1024]{1,0:T(8,128)(2,1)} %constant.5.clone.second_hbm) | copy-start | bytes 6291460
  19.4 24.3 %copy-start.1 = (f32[1,512,512]{2,1,0:T(8,128)S(1)}, f32[1,512,512]{2,1,0:T(8,128)}, u32[]{:S(2)}) copy-start(f32[1,512,512]{2,1,0:T(8,128)} %param.11) | copy-start | bytes 3145732
  19.6 1.3 %copy-start.2 = (bf16[512,1024]{1,0:T(8,128)(2,1)S(1)}, bf16[512,1024]{1,0:T(8,128)(2,1)}, u32[]{:S(2)}) copy-start(bf16[512,1024]{1,0:T(8,128)(2,1)} %constant.4.clone.first_hbm) | copy-start | bytes 3145732
  41.7 3.4 %collective-permute-start.2 = (bf16[112,1024]{1,0:T(8,128)(2,1)S(1)}, bf16[112,1024]{1,0:T(8,128)(2,1)S(1)}, u32[]{:S(2)}, u32[]{:S(2)}) collective-permute-start(bf16[112,1024]{1,0:T(8,128)(2,1)S(1)} %get-tuple-element.33), channel_id=1, source_target_pairs={{0,8},{1,9},{2,10},{3,11},{4,12},{5,13},{6,14},{7,15}} | collective-permute-start | bytes 688136 | tf_op jit(solution)/shard_map/ppermute | solution.py:306
  42.4 3.4 %collective-permute-start.1 = (bf16[112,1024]{1,0:T(8,128)(2,1)S(1)}, bf16[112,1024]{1,0:T(8,128)(2,1)S(1)}, u32[]{:S(2)}, u32[]{:S(2)}) collective-permute-start(bf16[112,1024]{1,0:T(8,128)(2,1)S(1)} %get-tuple-element.32), channel_id=1, source_target_pairs={{0,8},{1,9},{2,10},{3,11},{4,12},{5,13},{6,14},{7,15}} | collective-permute-start | bytes 688136 | tf_op jit(solution)/shard_map/ppermute | solution.py:306
  43.0 4.8 %collective-permute-start.6 = (bf16[112,1024]{1,0:T(8,128)(2,1)S(1)}, bf16[112,1024]{1,0:T(8,128)(2,1)S(1)}, u32[]{:S(2)}, u32[]{:S(2)}) collective-permute-start(bf16[112,1024]{1,0:T(8,128)(2,1)S(1)} %get-tuple-element.39), channel_id=1, source_target_pairs={{0,8},{1,9},{2,10},{3,11},{4,12},{5,13},{6,14},{7,15}} | collective-permute-start | bytes 688136 | tf_op jit(solution)/shard_map/ppermute | solution.py:306
  45.1 3.5 %collective-permute-start.5 = (bf16[112,1024]{1,0:T(8,128)(2,1)S(1)}, bf16[112,1024]{1,0:T(8,128)(2,1)S(1)}, u32[]{:S(2)}, u32[]{:S(2)}) collective-permute-start(bf16[112,1024]{1,0:T(8,128)(2,1)S(1)} %get-tuple-element.38), channel_id=1, source_target_pairs={{8,16},{9,17},{10,18},{11,19},{12,20},{13,21},{14,22},{15,23}} | collective-permute-start | bytes 688136 | tf_op jit(solution)/shard_map/ppermute | solution.py:306
  45.8 4.1 %collective-permute-start.3 = (bf16[112,1024]{1,0:T(8,128)(2,1)S(1)}, bf16[112,1024]{1,0:T(8,128)(2,1)S(1)}, u32[]{:S(2)}, u32[]{:S(2)}) collective-permute-start(bf16[112,1024]{1,0:T(8,128)(2,1)S(1)} %get-tuple-element.36), channel_id=1, source_target_pairs={{8,16},{9,17},{10,18},{11,19},{12,20},{13,21},{14,22},{15,23}} | collective-permute-start | bytes 688136 | tf_op jit(solution)/shard_map/ppermute | solution.py:306
  46.5 3.4 %collective-permute-start.4 = (bf16[96,1024]{1,0:T(8,128)(2,1)S(1)}, bf16[96,1024]{1,0:T(8,128)(2,1)S(1)}, u32[]{:S(2)}, u32[]{:S(2)}) collective-permute-start(bf16[96,1024]{1,0:T(8,128)(2,1)S(1)} %get-tuple-element.37), channel_id=1, source_target_pairs={{0,8},{1,9},{2,10},{3,11},{4,12},{5,13},{6,14},{7,15}} | collective-permute-start | bytes 589832 | tf_op jit(solution)/shard_map/ppermute | solution.py:306
  47.2 4.8 %collective-permute-start = (bf16[80,1024]{1,0:T(8,128)(2,1)S(1)}, bf16[80,1024]{1,0:T(8,128)(2,1)S(1)}, u32[]{:S(2)}, u32[]{:S(2)}) collective-permute-start(bf16[80,1024]{1,0:T(8,128)(2,1)S(1)} %get-tuple-element.31), channel_id=1, source_target_pairs={{0,8},{1,9},{2,10},{3,11},{4,12},{5,13},{6,14},{7,15}} | collective-permute-start | bytes 491528 | tf_op jit(solution)/shard_map/ppermute | solution.py:306
  47.9 4.8 %collective-permute-start.11 = (bf16[112,1024]{1,0:T(8,128)(2,1)S(1)}, bf16[112,1024]{1,0:T(8,128)(2,1)S(1)}, u32[]{:S(2)}, u32[]{:S(2)}) collective-permute-start(bf16[112,1024]{1,0:T(8,128)(2,1)S(1)} %get-tuple-element.49), channel_id=1, source_target_pairs={{8,16},{9,17},{10,18},{11,19},{12,20},{13,21},{14,22},{15,23}} | collective-permute-start | bytes 688136 | tf_op jit(solution)/shard_map/ppermute | solution.py:306
  48.6 21.4 %collective-permute-start.10 = (bf16[112,1024]{1,0:T(8,128)(2,1)S(1)}, bf16[112,1024]{1,0:T(8,128)(2,1)S(1)}, u32[]{:S(2)}, u32[]{:S(2)}) collective-permute-start(bf16[112,1024]{1,0:T(8,128)(2,1)S(1)} %get-tuple-element.48), channel_id=1, source_target_pairs={{16,24},{17,25},{18,26},{19,27},{20,28},{21,29},{22,30},{23,31}} | collective-permute-start | bytes 688136 | tf_op jit(solution)/shard_map/ppermute | solution.py:306
  50.0 24.9 %collective-permute-start.8 = (bf16[112,1024]{1,0:T(8,128)(2,1)S(1)}, bf16[112,1024]{1,0:T(8,128)(2,1)S(1)}, u32[]{:S(2)}, u32[]{:S(2)}) collective-permute-start(bf16[112,1024]{1,0:T(8,128)(2,1)S(1)} %get-tuple-element.46), channel_id=1, source_target_pairs={{16,24},{17,25},{18,26},{19,27},{20,28},{21,29},{22,30},{23,31}} | collective-permute-start | bytes 688136 | tf_op jit(solution)/shard_map/ppermute | solution.py:306
  51.3 19.0 %collective-permute-start.9 = (bf16[96,1024]{1,0:T(8,128)(2,1)S(1)}, bf16[96,1024]{1,0:T(8,128)(2,1)S(1)}, u32[]{:S(2)}, u32[]{:S(2)}) collective-permute-start(bf16[96,1024]{1,0:T(8,128)(2,1)S(1)} %get-tuple-element.47), channel_id=1, source_target_pairs={{8,16},{9,17},{10,18},{11,19},{12,20},{13,21},{14,22},{15,23}} | collective-permute-start | bytes 589832 | tf_op jit(solution)/shard_map/ppermute | solution.py:306
  52.0 23.1 %collective-permute-start.7 = (bf16[80,1024]{1,0:T(8,128)(2,1)S(1)}, bf16[80,1024]{1,0:T(8,128)(2,1)S(1)}, u32[]{:S(2)}, u32[]{:S(2)}) collective-permute-start(bf16[80,1024]{1,0:T(8,128)(2,1)S(1)} %get-tuple-element.45), channel_id=1, source_target_pairs={{8,16},{9,17},{10,18},{11,19},{12,20},{13,21},{14,22},{15,23}} | collective-permute-start | bytes 491528 | tf_op jit(solution)/shard_map/ppermute | solution.py:306
  52.7 27.1 %collective-permute-start.14 = (bf16[112,1024]{1,0:T(8,128)(2,1)S(1)}, bf16[112,1024]{1,0:T(8,128)(2,1)S(1)}, u32[]{:S(2)}, u32[]{:S(2)}) collective-permute-start(bf16[112,1024]{1,0:T(8,128)(2,1)S(1)} %get-tuple-element.55), channel_id=1, source_target_pairs={{16,24},{17,25},{18,26},{19,27},{20,28},{21,29},{22,30},{23,31}} | collective-permute-start | bytes 688136 | tf_op jit(solution)/shard_map/ppermute | solution.py:306
  70.3 13.4 %collective-permute-start.13 = (bf16[96,1024]{1,0:T(8,128)(2,1)S(1)}, bf16[96,1024]{1,0:T(8,128)(2,1)S(1)}, u32[]{:S(2)}, u32[]{:S(2)}) collective-permute-start(bf16[96,1024]{1,0:T(8,128)(2,1)S(1)} %get-tuple-element.54), channel_id=1, source_target_pairs={{16,24},{17,25},{18,26},{19,27},{20,28},{21,29},{22,30},{23,31}} | collective-permute-start | bytes 589832 | tf_op jit(solution)/shard_map/ppermute | solution.py:306
  75.1 10.3 %collective-permute-start.12 = (bf16[80,1024]{1,0:T(8,128)(2,1)S(1)}, bf16[80,1024]{1,0:T(8,128)(2,1)S(1)}, u32[]{:S(2)}, u32[]{:S(2)}) collective-permute-start(bf16[80,1024]{1,0:T(8,128)(2,1)S(1)} %get-tuple-element.53), channel_id=1, source_target_pairs={{16,24},{17,25},{18,26},{19,27},{20,28},{21,29},{22,30},{23,31}} | collective-permute-start | bytes 491528 | tf_op jit(solution)/shard_map/ppermute | solution.py:306

commit v3 on v2

v3 whole, which is shorter than its diff:
```python
import functools
import math

import jax
import jax.numpy as jnp
import numpy as np
from jax import lax
from jax.experimental import pallas as pl
from jax.experimental.pallas import tpu as pltpu
from jax.sharding import PartitionSpec as P

SUB = 64
LANES = 128
ROWS = 8
GROUP = 8
PARTS = (7, 7, 7, 6, 5)
AHEAD = 2
LAG = 2
DIGITS = 3
DIGIT = 16.0
SINE = tuple(
    float(v)
    for v in np.linalg.lstsq(
        *(
            lambda x, w: (
                (x[:, None] ** np.arange(1, 10, 2)[None, :]) * w[:, None],
                np.sin(2 * np.pi * x) * w,
            )
        )(
            0.5 * np.cos(np.pi * (np.arange(2000) + 0.5) / 4000),
            np.ones(2000),
        ),
        rcond=None,
    )[0]
)


def sine_turns(turns):
    x = turns - jnp.round(turns)
    x2 = x * x
    total = jnp.full_like(x, SINE[-1])
    for c in SINE[-2::-1]:
        total = total * x2 + c
    return total * x


def pack_kernel(owners, cap, routes, offsets, angles, vis, out, counts, angle_rows, vis_rows):
    out[...] = jnp.zeros_like(out)
    angle_rows[...] = angles[...].T
    values = vis[...].astype(jnp.float32)
    spot = lax.broadcasted_iota(jnp.int32, values.shape, 0)
    for axis in range(2):
        for place in range(DIGITS):
            digit = (offsets[axis : axis + 1, :] >> (3 * place)) & 7
            carried = jnp.where(spot == axis * DIGITS + place, digit, 0)
            values = values + carried.astype(jnp.float32) * DIGIT
    vis_rows[...] = values.T

    def clear(i, _):
        counts[i] = 0
        return 0

    lax.fori_loop(0, owners, clear, 0)

    def place_row(i, _):
        owner = routes[0, i]
        rank = counts[owner]
        counts[owner] = rank + 1
        base = owner * (2 * cap) + rank
        out[pl.ds(base, 1), :] = angle_rows[pl.ds(i, 1), :]
        out[pl.ds(base + cap, 1), :] = vis_rows[pl.ds(i, 1), :]
        return 0

    lax.fori_loop(0, angles.shape[1], place_row, 0, unroll=8)


def pack(routes, offsets, angles, vis, owners, cap):
    smem = pl.BlockSpec(memory_space=pltpu.SMEM)
    vmem = pl.BlockSpec(memory_space=pltpu.VMEM)
    return pl.pallas_call(
        functools.partial(pack_kernel, owners, cap),
        out_shape=jax.ShapeDtypeStruct((owners * cap * 2, LANES), jnp.float32),
        in_specs=[smem, vmem, vmem, vmem],
        out_specs=vmem,
        scratch_shapes=[
            pltpu.SMEM((owners,), jnp.int32),
            pltpu.VMEM(angles.shape[::-1], jnp.float32),
            pltpu.VMEM(vis.shape[::-1], jnp.float32),
        ],
        name="pack",
    )(routes, offsets, angles, vis)


def grid_kernel(
    owners, offsets, got, first_hbm, second_hbm, dense, first, second,
    turns_u, turns_v, amp_a, amp_b, grid, sems, *stages,
):
    slots = got.shape[0] // 2
    cap = slots // owners
    grid_n = dense.shape[0]
    blocks = grid_n // SUB
    group = stages[0].shape[0]
    groups = slots // group
    bases, lefts, rights, pieces = (stages[2 * k : 2 * k + 2] for k in range(4))
    copies = [
        pltpu.make_async_copy(first_hbm, first, sems.at[0]),
        pltpu.make_async_copy(second_hbm, second, sems.at[1]),
    ]
    for copy in copies:
        copy.start()

    lane = lax.broadcasted_iota(jnp.int32, (ROWS, LANES), 1)
    low = lane < SUB
    row = lax.broadcasted_iota(jnp.int32, (ROWS, LANES), 0)
    quarter = jnp.where(low, 0.25, 0.0).astype(jnp.float32)
    sign = jnp.where(low, -1.0, 1.0).astype(jnp.float32)
    row_f = row.astype(jnp.float32)
    upper = row < ROWS // 2
    eights = ((row & (ROWS // 2 - 1)) * ROWS + ROWS).astype(jnp.float32)
    middle = SUB // ROWS // 2

    low_cap = lax.broadcasted_iota(jnp.int32, (cap, LANES), 1) < SUB

    def spread_out(i, _):
        angles = got[pl.ds(i * (2 * cap), cap), :]
        vis = got[pl.ds(i * (2 * cap) + cap, cap), :]
        vis = vis - jnp.round(vis * (1.0 / DIGIT)) * DIGIT
        rows = pl.ds(i * cap, cap)
        both = angles * (1.0 / (2.0 * math.pi))
        swapped = pltpu.roll(both, SUB, 1)
        turns_u[rows, :] = jnp.where(low_cap, both, swapped)
        turns_v[rows, :] = jnp.where(low_cap, swapped, both)
        both = vis * (1.0 / math.sqrt(SUB))
        swapped = pltpu.roll(both, SUB, 1)
        amp_a[rows, :] = jnp.where(low_cap, both, swapped)
        amp_b[rows, :] = jnp.where(low_cap, swapped, both)
        return 0

    lax.fori_loop(0, owners, spread_out, 0, unroll=8)

    def clear(b, _):
        grid[b] = jnp.zeros(grid.shape[1:], grid.dtype)
        return 0

    lax.fori_loop(0, blocks + 1, clear, 0)

    def spread(ref, s):
        return jnp.broadcast_to(ref[pl.ds(s, 1), :], (ROWS, LANES))

    def find_bases(g, out):
        for i in range(group):
            s = g * group + i
            tu, tv = spread(turns_u, s), spread(turns_v, s)
            a, b = spread(amp_a, s), spread(amp_b, s)
            cs = sine_turns(tu * row_f + quarter)
            sc = pltpu.roll(cs, SUB, 1) * sign
            out[i, 0] = cs * a + sc * b
            out[i, 1] = sc * a - cs * b
            cs = sine_turns(tv * row_f + quarter)
            out[i, 2] = -(cs * sign)
            out[i, 3] = pltpu.roll(cs, SUB, 1)
            cs = sine_turns(jnp.where(upper, tu, tv) * eights + quarter)
            sc = pltpu.roll(cs, SUB, 1)
            out[i, 4] = jnp.where(low, cs, sc)
            out[i, 5] = jnp.where(low, sc, cs)

    def find_rows(source, left, right):
        for i in range(group):

            def line(k, j):
                return jnp.broadcast_to(source[i, k, j : j + 1, :], (ROWS, LANES))

            x, y = source[i, 0], source[i, 1]
            parts = [x]
            for j in range(middle):
                along, across = x * line(4, j), y * line(5, j)
                parts = [along - across] + parts
                if j + 1 < middle:
                    parts = parts + [along + across]
            left[i] = jnp.concatenate(parts, axis=0).astype(jnp.bfloat16)

            def keep(k, value_re, value_im):
                places = (0, 2 * middle) if k == 0 else (k,)
                for place in places:
                    right[i, 0, place * ROWS : (place + 1) * ROWS, :] = value_re
                    right[i, 1, place * ROWS : (place + 1) * ROWS, :] = value_im

            x, y = source[i, 2], source[i, 3]
            keep(middle, x, y)
            for j in range(middle):
                wr, wi = line(4, middle + j), line(5, middle + j)
                xr, xi, yr, yi = x * wr, x * wi, y * wr, y * wi
                keep(middle - 1 - j, xr + yi, yr - xi)
                if j + 1 < middle:
                    keep(middle + 1 + j, xr - yi, yr + xi)

    def multiply(g, left, right, out):
        for i in range(group):
            shift = offsets[2 * (g * group + i) + 1] & (SUB - 1)
            parts = [
                right[i, k, pl.ds((j * ROWS - shift) & (SUB - 1), ROWS), :]
                for k in range(2)
                for j in range(SUB // ROWS)
            ]
            turned = jnp.concatenate(parts, axis=0).astype(jnp.bfloat16)
            out[i] = lax.dot_general(
                left[i], turned, (((1,), (1,)), ((), ())), preferred_element_type=jnp.float32
            )

    cell = lane & (SUB - 1)

    def add(g, formed):
        for i in range(group):
            s = g * group + i
            off_u, off_v = offsets[2 * s], offsets[2 * s + 1]
            block = off_v // SUB
            here = cell >= (off_v & (SUB - 1))
            for side in range(2):
                for j in range(SUB // ROWS):
                    place = grid.at[block + side, pl.ds(off_u + j * ROWS, ROWS), :]
                    total = place[...] + formed[i, j * ROWS : (j + 1) * ROWS, :]
                    pltpu.store(place, total, mask=~here if side else here)

    pieces[0][...] = jnp.zeros_like(pieces[0])
    lefts[1][...] = jnp.zeros_like(lefts[1])
    rights[1][...] = jnp.zeros_like(rights[1])
    find_bases(0, bases[0])

    def pair(p, _):
        for k in range(2):
            g = 2 * p + k
            add(jnp.maximum(g - 2, 0), pieces[k])
            multiply(jnp.maximum(g - 1, 0), lefts[1 - k], rights[1 - k], pieces[1 - k])
            find_rows(bases[k], lefts[k], rights[k])
            find_bases(jnp.minimum(g + 1, groups - 1), bases[1 - k])
        return 0

    lax.fori_loop(0, groups // 2, pair, 0)
    add(groups - 2, pieces[0])
    multiply(groups - 1, lefts[1], rights[1], pieces[1])
    add(groups - 1, pieces[1])

    for b in range(blocks):
        dense[:, b * LANES : (b + 1) * LANES] = grid[b].astype(jnp.bfloat16)
    for copy in copies:
        copy.wait()


def form_grid(offsets, got, first, second, owners):
    slots = got.shape[0] // 2
    grid_n = first.shape[0]
    blocks = grid_n // SUB
    group = math.gcd(slots // 2, GROUP)
    smem = pl.BlockSpec(memory_space=pltpu.SMEM)
    vmem = pl.BlockSpec(memory_space=pltpu.VMEM)
    hbm = pl.BlockSpec(memory_space=pltpu.HBM)
    line = pltpu.VMEM((slots, LANES), jnp.float32)
    stages = [
        pltpu.VMEM((group, 6, ROWS, LANES), jnp.float32),
        pltpu.VMEM((group, SUB, LANES), jnp.bfloat16),
        pltpu.VMEM((group, 2, SUB + ROWS, LANES), jnp.float32),
        pltpu.VMEM((group, SUB, LANES), jnp.float32),
    ]
    return pl.pallas_call(
        functools.partial(grid_kernel, owners),
        out_shape=[
            pltpu.VMEM((grid_n, 2 * grid_n), jnp.bfloat16),
            pltpu.VMEM(first.shape, jnp.bfloat16),
            pltpu.VMEM(second.shape, jnp.bfloat16),
        ],
        in_specs=[smem, vmem, hbm, hbm],
        out_specs=[vmem] * 3,
        scratch_shapes=[
            line, line, line, line,
            pltpu.VMEM((blocks + 1, grid_n, LANES), jnp.float32),
            pltpu.SemaphoreType.DMA((2,)),
            *(stage for stage in stages for _ in range(2)),
        ],
        compiler_params=pltpu.CompilerParams(vmem_limit_bytes=24 * 1024 * 1024),
        name="grid",
    )(
        offsets,
        got,
        pltpu.with_memory_space_constraint(first, pltpu.HBM),
        pltpu.with_memory_space_constraint(second, pltpu.HBM),
    )


def transform_rows(dense, first, second, start, end):
    grid_n = dense.shape[0]
    rows = end - start
    both = jnp.concatenate([first[start:end, :grid_n], first[start:end, grid_n:]], axis=0)
    both = jnp.dot(both, dense[...], preferred_element_type=jnp.float32)
    sign = jnp.where(lax.broadcasted_iota(jnp.int32, (rows, LANES), 1) < SUB, -1.0, 1.0)
    half = [
        both[:rows, at : at + LANES] + pltpu.roll(both[rows:, at : at + LANES], SUB, 1) * sign
        for at in range(0, 2 * grid_n, LANES)
    ]
    half = jnp.concatenate(half, axis=1).astype(jnp.bfloat16)
    return jnp.dot(half, second[...], preferred_element_type=jnp.float32)


def first_rows_kernel(end, dense, first, second, image, send):
    rows = transform_rows(dense, first, second, 0, end)
    image[0:end, :] = rows
    send[...] = rows.astype(jnp.bfloat16)


def turn_rows(phase, turns, start, end):
    grid_n = phase.shape[1]
    part = phase[start:end, :] * (1.0 / (2.0 * math.pi))
    turns[start:end, :grid_n] = sine_turns(part + 0.25)
    turns[start:end, grid_n:] = sine_turns(part)


def other_rows_kernel(bounds, phase, dense, first, second, _, image, turns):
    turn_rows(phase, turns, 0, bounds[1])
    for start, end in zip(bounds[1:], bounds[2:]):
        image[start:end, :] = transform_rows(dense, first, second, start, end)
        turn_rows(phase, turns, start, end)


def pinned(*arrays):
    return [pltpu.with_memory_space_constraint(x, pltpu.VMEM) for x in arrays]


def first_rows(dense, first, second, end):
    grid_n = first.shape[0]
    vmem = pl.BlockSpec(memory_space=pltpu.VMEM)
    return pl.pallas_call(
        functools.partial(first_rows_kernel, end),
        out_shape=[
            pltpu.VMEM((grid_n, 2 * grid_n), jnp.float32),
            pltpu.VMEM((end, 2 * grid_n), jnp.bfloat16),
        ],
        in_specs=[vmem] * 3,
        out_specs=[vmem] * 2,
        compiler_params=pltpu.CompilerParams(vmem_limit_bytes=8 * 1024 * 1024),
        name="first_rows",
    )(*pinned(dense, first, second))


def other_rows(phase, dense, first, second, image, bounds):
    vmem = pl.BlockSpec(memory_space=pltpu.VMEM)
    return pl.pallas_call(
        functools.partial(other_rows_kernel, bounds),
        out_shape=[pltpu.VMEM(image.shape, jnp.float32), pltpu.VMEM(image.shape, jnp.float32)],
        in_specs=[vmem] * 5,
        out_specs=[vmem] * 2,
        input_output_aliases={4: 0},
        compiler_params=pltpu.CompilerParams(vmem_limit_bytes=8 * 1024 * 1024),
        name="other_rows",
    )(*pinned(phase, dense, first, second, image))


def dft_tables(grid_n):
    line = np.arange(grid_n)
    angle = (line[:, None] * line[None, :] % grid_n) * (2.0 * np.pi / grid_n)
    cos = np.cos(angle) / math.sqrt(grid_n)
    sin = np.sin(angle) / math.sqrt(grid_n)
    first = np.concatenate([cos, sin], axis=1)
    real = np.concatenate([cos, sin], axis=1).reshape(grid_n // SUB, SUB, 2 * grid_n)
    imag = np.concatenate([-sin, cos], axis=1).reshape(grid_n // SUB, SUB, 2 * grid_n)
    second = np.concatenate([real, imag], axis=1).reshape(2 * grid_n, 2 * grid_n)
    return first.astype(np.float32).astype(jnp.bfloat16), second.astype(np.float32).astype(jnp.bfloat16)


def send_up(part, hop):
    return lax.ppermute(part, "wa", [(hop - 1, hop)])


def horner_kernel(hop, start, incoming, image, turns, *outs):
    grid_n = image.shape[1] // 2
    rows = pl.ds(start, incoming.shape[0])
    re_cells, im_cells = pl.ds(0, grid_n), pl.ds(grid_n, grid_n)

    @pl.when(lax.axis_index("wa") == hop)
    def _():
        re = incoming[:, re_cells].astype(jnp.float32)
        im = incoming[:, im_cells].astype(jnp.float32)
        turn_re, turn_im = turns[rows, re_cells], turns[rows, im_cells]
        new_re = turn_re * re - turn_im * im + image[rows, re_cells]
        new_im = turn_re * im + turn_im * re + image[rows, im_cells]
        outs[-1][rows, re_cells] = new_re
        outs[-1][rows, im_cells] = new_im
        for send in outs[:-1]:
            send[:, re_cells] = new_re.astype(jnp.bfloat16)
            send[:, im_cells] = new_im.astype(jnp.bfloat16)


def horner_step(hop, planes, start, end, incoming, image, turns):
    vmem = pl.BlockSpec(memory_space=pltpu.VMEM)
    outs = [pltpu.VMEM((end - start, image.shape[1]), jnp.bfloat16)] * (hop + 1 < planes)
    outs.append(pltpu.VMEM(image.shape, jnp.float32))
    got = pl.pallas_call(
        functools.partial(horner_kernel, hop, start),
        out_shape=outs,
        in_specs=[vmem] * 3,
        out_specs=[vmem] * len(outs),
        input_output_aliases={1: len(outs) - 1},
        compiler_params=pltpu.CompilerParams(vmem_limit_bytes=4 * 1024 * 1024),
        name="horner",
    )(*pinned(incoming, image, turns))
    return got[0], got[-1]


def begin_kernel(start, image, send, _):
    @pl.when(lax.axis_index("wa") == 0)
    def _():
        send[...] = image[pl.ds(start, send.shape[0]), :].astype(jnp.bfloat16)


def begin_chain(start, end, image):
    vmem = pl.BlockSpec(memory_space=pltpu.VMEM)
    return pl.pallas_call(
        functools.partial(begin_kernel, start),
        out_shape=[
            pltpu.VMEM((end - start, image.shape[1]), jnp.bfloat16),
            pltpu.VMEM(image.shape, jnp.float32),
        ],
        in_specs=[vmem],
        out_specs=[vmem] * 2,
        input_output_aliases={0: 1},
        compiler_params=pltpu.CompilerParams(vmem_limit_bytes=4 * 1024 * 1024),
        name="begin",
    )(*pinned(image))


def on_device(visibilities, uv_angles, routes, offsets, pixel_phase):
    sub_count = visibilities.shape[0]
    count_vis = visibilities.shape[2]
    grid_n = pixel_phase.shape[1]
    planes = lax.axis_size("wa")
    owners = planes * lax.axis_size("facet")
    cap = max(2, (2 * sub_count + owners - 1) // owners)
    slots = owners * cap
    sent = pack(
        routes.T,
        offsets.T,
        uv_angles.transpose(1, 2, 0).reshape(2 * count_vis, sub_count),
        visibilities.transpose(1, 2, 0).reshape(2 * count_vis, sub_count),
        owners,
        cap,
    )
    got = lax.all_to_all(sent, ("wa", "facet"), split_axis=0, concat_axis=0, tiled=True)
    digits = got.reshape(owners, 2, cap, LANES)[:, 1, :, : 2 * DIGITS]
    digits = jnp.round(digits * (1.0 / DIGIT)).astype(jnp.int32).reshape(slots, 2, DIGITS)
    own_offsets = digits[:, :, 0]
    for place in range(1, DIGITS):
        own_offsets = own_offsets + (digits[:, :, place] << (3 * place))
    first, second = (jnp.asarray(x) for x in dft_tables(grid_n))
    dense, first, second = form_grid(own_offsets.reshape(2 * slots), got, first, second, owners)

    units = grid_n // 16
    bounds = [0] + [16 * (units * sum(PARTS[: i + 1]) // sum(PARTS)) for i in range(len(PARTS))]
    count = len(PARTS)
    image, send = first_rows(dense, first, second, bounds[1])
    incoming = {(1, 0): send_up(send, 1)}
    image, turns = other_rows(pixel_phase[0], dense, first, second, image, bounds)

    def begin(c, image):
        if c < count:
            send, image = begin_chain(bounds[c], bounds[c + 1], image)
            incoming[1, c] = send_up(send, 1)
        return image

    for c in range(1, AHEAD):
        image = begin(c, image)
    for beat in range(count + LAG * planes):
        for hop in range(1, planes):
            c = beat - LAG * (hop - 1)
            if 0 <= c < count:
                send, image = horner_step(
                    hop, planes, bounds[c], bounds[c + 1], incoming[hop, c], image, turns
                )
                if hop + 1 < planes:
                    incoming[hop + 1, c] = send_up(send, hop + 1)
                if hop == 1:
                    image = begin(c + AHEAD, image)
    return image.reshape(1, 1, grid_n, 2 * grid_n)


def solution(mesh):
    in_specs = (
        P(("wa", "facet"), None, None),
        P(("wa", "facet"), None, None),
        P(("wa", "facet"), None),
        P(("wa", "facet"), None),
        P("facet", None, None),
    )
    out_specs = P("wa", "facet", None, None)
    return jax.shard_map(
        on_device, mesh=mesh, in_specs=in_specs, out_specs=out_specs, check_vma=False
    )
```

time: 87.3 us -> 75.1 us (0.86)
  the two profiles are of different devices: /device:TPU:24 before, /device:TPU:26 now
where the time goes in v3:
time: 75.1 us; the launch traced here: 74.7 us
  waiting for transfers between devices  26.5 us (35%)
  Pallas kernels  19.4 us (26%)
  blocking collectives  13.3 us (18%)
  starting transfers between devices  13.2 us (18%)
  local copies, waits for them, and re-layouts  1.95 us (3%)
    ppermute x15, waiting for transfers between devices, send_up(): return lax.ppermute(part, 'wa', [(hop - 1, hop)])  26.5 us
    all_to_all x1, blocking collectives, on_device(): lax.all_to_all(sent, ('wa', 'facet'), split_axis=0, concat_axis=0, tiled=...  13.3 us
    ppermute x15, starting transfers between devices, send_up(): return lax.ppermute(part, 'wa', [(hop - 1, hop)])  13.2 us
    pallas_call x1, Pallas kernels, form_grid(): pl.pallas_call(functools.partial(grid_kernel, owners), out_shape=[pltpu.V...  10.9 us
    pallas_call x1, Pallas kernels, other_rows(): pl.pallas_call(functools.partial(other_rows_kernel, bounds), out_shape=[p...  3.96 us
    pallas_call x1, Pallas kernels, pack(): pl.pallas_call(functools.partial(pack_kernel, owners, cap), out_shape=jax...  2.45 us
  transfers between devices with their start and end apart: 15, of which 5 were waited for; matrix products, arithmetic and copies ran while one was open for 0% of the time, Pallas kernels for 7%

profile of v3, /device:TPU:26, one launch (start us, length us, event | category | flops | bytes accessed | tf_op | source)
XLA Modules:
  0.0 74.7 jit_solution(2521641441557303458)
XLA Ops:
  0.0 2.4 %pack.1 = f32[512,128]{1,0:T(8,128)} custom-call(s32[1,128]{1,0:T(1,128)} %bitcast.27, s32[2,128]{1,0:T(2,128)} %bitcast.26, f32[128,128]{1,0:T(8,128)} %bitcast.24, bf16[128,128]{1,0:T(8,128)(2,1)} %bitcast.25), custom_call_target="tpu_custom_call" | custom-call | tf_op jit(solution)/shard_map/pack/pallas_call | solution.py:80
  2.4 13.3 %all_to_all.11 = f32[32,16,128]{2,1,0:T(8,128)S(1)} all-to-all(f32[32,16,128]{2,1,0:T(8,128)} %bitcast.23), channel_id=1, replica_groups=mesh['wa'=4,'facet'=8] {'wa','facet'}, dimensions={0} | all-to-all | bytes 524288 | tf_op jit(solution)/shard_map/all_to_all | solution.py:445
  16.2 0.1 add.14.offsets
  16.4 10.9 %grid.1 = (bf16[512,1024]{1,0:T(8,128)(2,1)S(1)}, bf16[512,1024]{1,0:T(8,128)(2,1)S(1)}, bf16[1024,1024]{1,0:T(8,128)(2,1)S(1)}) custom-call(s32[512]{0:T(512)S(1)} %add.14.offsets, f32[512,128]{1,0:T(8,128)S(1)} %bitcast.21, bf16[512,1024]{1,0:T(8,128)(2,1)} %constant.10.clone.first_hbm, bf16[1024,1024]{1,0:T(8,128)(2,1)} %constant.11.clone.second_hbm), custom_call_target="tpu_custom_call" | custom-call | tf_op jit(solution)/shard_map/grid/pallas_call | solution.py:264
  27.3 0.8 %first_rows.1 = (f32[512,1024]{1,0:T(8,128)S(1)}, bf16[112,1024]{1,0:T(8,128)(2,1)S(1)}) custom-call(bf16[512,1024]{1,0:T(8,128)(2,1)S(1)} %get-tuple-element.40.dense, bf16[512,1024]{1,0:T(8,128)(2,1)S(1)} %get-tuple-element.41.first, bf16[1024,1024]{1,0:T(8,128)(2,1)S(1)} %get-tuple-element.42.second), custom_call_target="tpu_custom_call" | custom-call | tf_op jit(solution)/shard_map/first_rows/pallas_call | solution.py:330
  28.2 0.7 collective-permute-start
  28.9 4.0 %other_rows.1 = (f32[512,1024]{1,0:T(8,128)S(1)}, f32[512,1024]{1,0:T(8,128)S(1)}) custom-call(f32[512,512]{1,0:T(8,128)S(1)} %bitcast.22, bf16[512,1024]{1,0:T(8,128)(2,1)S(1)} %get-tuple-element.40.dense, bf16[512,1024]{1,0:T(8,128)(2,1)S(1)} %get-tuple-element.41.first, ...), custom_call_target="tpu_custom_call", output_to_operand_aliasing={{0}: (4, {})} | custom-call | tf_op jit(solution)/shard_map/other_rows/pallas_call | solution.py:345
  32.9 0.7 collective-permute-start.2
  33.6 0.7 collective-permute-start.1
  34.3 0.7 collective-permute-start.6
  35.0 0.7 collective-permute-start.4
  35.7 0.7 collective-permute-start.5
  36.5 0.7 collective-permute-start.3
  37.1 0.7 collective-permute-start.11
  37.9 1.3 %collective-permute-start.10 = (bf16[112,1024]{1,0:T(8,128)(2,1)S(1)}, bf16[112,1024]{1,0:T(8,128)(2,1)S(1)}, u32[]{:S(2)}, u32[]{:S(2)}) collective-permute-start(bf16[112,1024]{1,0:T(8,128)(2,1)S(1)} %get-tuple-element.66), channel_id=1, source_target_pairs={{16,24},{17,25},{18,26},{19,27},{20,28},{21,29},{22,30},{23,31}} | collective-permute-start | bytes 688136 | tf_op jit(solution)/shard_map/ppermute | solution.py:369
  39.2 1.3 %collective-permute-start.8 = (bf16[112,1024]{1,0:T(8,128)(2,1)S(1)}, bf16[112,1024]{1,0:T(8,128)(2,1)S(1)}, u32[]{:S(2)}, u32[]{:S(2)}) collective-permute-start(bf16[112,1024]{1,0:T(8,128)(2,1)S(1)} %get-tuple-element.64), channel_id=1, source_target_pairs={{16,24},{17,25},{18,26},{19,27},{20,28},{21,29},{22,30},{23,31}} | collective-permute-start | bytes 688136 | tf_op jit(solution)/shard_map/ppermute | solution.py:369
  40.5 0.7 collective-permute-start.9
  41.3 0.7 collective-permute-start.7
  42.0 1.3 %collective-permute-start.14 = (bf16[112,1024]{1,0:T(8,128)(2,1)S(1)}, bf16[112,1024]{1,0:T(8,128)(2,1)S(1)}, u32[]{:S(2)}, u32[]{:S(2)}) collective-permute-start(bf16[112,1024]{1,0:T(8,128)(2,1)S(1)} %get-tuple-element.73), channel_id=1, source_target_pairs={{16,24},{17,25},{18,26},{19,27},{20,28},{21,29},{22,30},{23,31}} | collective-permute-start | bytes 688136 | tf_op jit(solution)/shard_map/ppermute | solution.py:369
  43.3 12.1 %collective-permute-done.10.incoming = bf16[112,1024]{1,0:T(8,128)(2,1)S(1)} collective-permute-done((bf16[112,1024]{1,0:T(8,128)(2,1)S(1)}, bf16[112,1024]{1,0:T(8,128)(2,1)S(1)}, u32[]{:S(2)}, u32[]{:S(2)}) %collective-permute-start.10) | collective-permute-done | bytes 229408 | tf_op jit(solution)/shard_map/ppermute | solution.py:369
  55.4 0.2 horner.23.image
  55.7 1.3 %collective-permute-start.13 = (bf16[96,1024]{1,0:T(8,128)(2,1)S(1)}, bf16[96,1024]{1,0:T(8,128)(2,1)S(1)}, u32[]{:S(2)}, u32[]{:S(2)}) collective-permute-start(bf16[96,1024]{1,0:T(8,128)(2,1)S(1)} %get-tuple-element.72), channel_id=1, source_target_pairs={{16,24},{17,25},{18,26},{19,27},{20,28},{21,29},{22,30},{23,31}} | collective-permute-start | bytes 589832 | tf_op jit(solution)/shard_map/ppermute | solution.py:369
  57.0 3.5 %collective-permute-done.8.incoming = bf16[112,1024]{1,0:T(8,128)(2,1)S(1)} collective-permute-done((bf16[112,1024]{1,0:T(8,128)(2,1)S(1)}, bf16[112,1024]{1,0:T(8,128)(2,1)S(1)}, u32[]{:S(2)}, u32[]{:S(2)}) %collective-permute-start.8) | collective-permute-done | bytes 229408 | tf_op jit(solution)/shard_map/ppermute | solution.py:369
  60.5 0.2 horner.25.image
  60.8 1.3 %collective-permute-start.12 = (bf16[80,1024]{1,0:T(8,128)(2,1)S(1)}, bf16[80,1024]{1,0:T(8,128)(2,1)S(1)}, u32[]{:S(2)}, u32[]{:S(2)}) collective-permute-start(bf16[80,1024]{1,0:T(8,128)(2,1)S(1)} %get-tuple-element.71), channel_id=1, source_target_pairs={{16,24},{17,25},{18,26},{19,27},{20,28},{21,29},{22,30},{23,31}} | collective-permute-start | bytes 491528 | tf_op jit(solution)/shard_map/ppermute | solution.py:369
  62.1 4.2 %collective-permute-done.14.incoming = bf16[112,1024]{1,0:T(8,128)(2,1)S(1)} collective-permute-done((bf16[112,1024]{1,0:T(8,128)(2,1)S(1)}, bf16[112,1024]{1,0:T(8,128)(2,1)S(1)}, u32[]{:S(2)}, u32[]{:S(2)}) %collective-permute-start.14) | collective-permute-done | bytes 229408 | tf_op jit(solution)/shard_map/ppermute | solution.py:369
  66.3 0.2 horner.27.image
  66.5 5.0 %collective-permute-done.13.incoming = bf16[96,1024]{1,0:T(8,128)(2,1)S(1)} collective-permute-done((bf16[96,1024]{1,0:T(8,128)(2,1)S(1)}, bf16[96,1024]{1,0:T(8,128)(2,1)S(1)}, u32[]{:S(2)}, u32[]{:S(2)}) %collective-permute-start.13) | collective-permute-done | bytes 196640 | tf_op jit(solution)/shard_map/ppermute | solution.py:369
  71.5 0.2 horner.28.image
  71.7 1.6 %collective-permute-done.12.incoming = bf16[80,1024]{1,0:T(8,128)(2,1)S(1)} collective-permute-done((bf16[80,1024]{1,0:T(8,128)(2,1)S(1)}, bf16[80,1024]{1,0:T(8,128)(2,1)S(1)}, u32[]{:S(2)}, u32[]{:S(2)}) %collective-permute-start.12) | collective-permute-done | bytes 163872 | tf_op jit(solution)/shard_map/ppermute | solution.py:369
  73.2 0.2 horner.29
  73.4 1.3 %copy.55 = f32[1,1,512,1024]{3,2,1,0:T(8,128)} copy(f32[1,1,512,1024]{3,2,1,0:T(8,128)S(1)} %bitcast.19) | data formatting | bytes 4194304
  (33 shorter events, 0.8 us)
Async XLA Ops:
  27.3 1.5 %copy-start = (f32[1,512,512]{2,1,0:T(8,128)S(1)}, f32[1,512,512]{2,1,0:T(8,128)}, u32[]{:S(2)}) copy-start(f32[1,512,512]{2,1,0:T(8,128)} %param.11) | copy-start | bytes 3145732
  28.2 5.4 %collective-permute-start = (bf16[112,1024]{1,0:T(8,128)(2,1)S(1)}, bf16[112,1024]{1,0:T(8,128)(2,1)S(1)}, u32[]{:S(2)}, u32[]{:S(2)}) collective-permute-start(bf16[112,1024]{1,0:T(8,128)(2,1)S(1)} %get-tuple-element.43), channel_id=1, source_target_pairs={{0,8},{1,9},{2,10},{3,11},{4,12},{5,13},{6,14},{7,15}} | collective-permute-start | bytes 688136 | tf_op jit(solution)/shard_map/ppermute | solution.py:369
  32.9 2.1 %collective-permute-start.2 = (bf16[112,1024]{1,0:T(8,128)(2,1)S(1)}, bf16[112,1024]{1,0:T(8,128)(2,1)S(1)}, u32[]{:S(2)}, u32[]{:S(2)}) collective-permute-start(bf16[112,1024]{1,0:T(8,128)(2,1)S(1)} %get-tuple-element.50), channel_id=1, source_target_pairs={{0,8},{1,9},{2,10},{3,11},{4,12},{5,13},{6,14},{7,15}} | collective-permute-start | bytes 688136 | tf_op jit(solution)/shard_map/ppermute | solution.py:369
  33.6 2.8 %collective-permute-start.1 = (bf16[112,1024]{1,0:T(8,128)(2,1)S(1)}, bf16[112,1024]{1,0:T(8,128)(2,1)S(1)}, u32[]{:S(2)}, u32[]{:S(2)}) collective-permute-start(bf16[112,1024]{1,0:T(8,128)(2,1)S(1)} %get-tuple-element.49), channel_id=1, source_target_pairs={{0,8},{1,9},{2,10},{3,11},{4,12},{5,13},{6,14},{7,15}} | collective-permute-start | bytes 688136 | tf_op jit(solution)/shard_map/ppermute | solution.py:369
  34.3 3.5 %collective-permute-start.6 = (bf16[112,1024]{1,0:T(8,128)(2,1)S(1)}, bf16[112,1024]{1,0:T(8,128)(2,1)S(1)}, u32[]{:S(2)}, u32[]{:S(2)}) collective-permute-start(bf16[112,1024]{1,0:T(8,128)(2,1)S(1)} %get-tuple-element.58), channel_id=1, source_target_pairs={{8,16},{9,17},{10,18},{11,19},{12,20},{13,21},{14,22},{15,23}} | collective-permute-start | bytes 688136 | tf_op jit(solution)/shard_map/ppermute | solution.py:369
  35.0 4.2 %collective-permute-start.4 = (bf16[112,1024]{1,0:T(8,128)(2,1)S(1)}, bf16[112,1024]{1,0:T(8,128)(2,1)S(1)}, u32[]{:S(2)}, u32[]{:S(2)}) collective-permute-start(bf16[112,1024]{1,0:T(8,128)(2,1)S(1)} %get-tuple-element.56), channel_id=1, source_target_pairs={{8,16},{9,17},{10,18},{11,19},{12,20},{13,21},{14,22},{15,23}} | collective-permute-start | bytes 688136 | tf_op jit(solution)/shard_map/ppermute | solution.py:369
  35.7 3.4 %collective-permute-start.5 = (bf16[96,1024]{1,0:T(8,128)(2,1)S(1)}, bf16[96,1024]{1,0:T(8,128)(2,1)S(1)}, u32[]{:S(2)}, u32[]{:S(2)}) collective-permute-start(bf16[96,1024]{1,0:T(8,128)(2,1)S(1)} %get-tuple-element.57), channel_id=1, source_target_pairs={{0,8},{1,9},{2,10},{3,11},{4,12},{5,13},{6,14},{7,15}} | collective-permute-start | bytes 589832 | tf_op jit(solution)/shard_map/ppermute | solution.py:369
  36.5 4.8 %collective-permute-start.3 = (bf16[80,1024]{1,0:T(8,128)(2,1)S(1)}, bf16[80,1024]{1,0:T(8,128)(2,1)S(1)}, u32[]{:S(2)}, u32[]{:S(2)}) collective-permute-start(bf16[80,1024]{1,0:T(8,128)(2,1)S(1)} %get-tuple-element.55), channel_id=1, source_target_pairs={{0,8},{1,9},{2,10},{3,11},{4,12},{5,13},{6,14},{7,15}} | collective-permute-start | bytes 491528 | tf_op jit(solution)/shard_map/ppermute | solution.py:369
  37.1 4.8 %collective-permute-start.11 = (bf16[112,1024]{1,0:T(8,128)(2,1)S(1)}, bf16[112,1024]{1,0:T(8,128)(2,1)S(1)}, u32[]{:S(2)}, u32[]{:S(2)}) collective-permute-start(bf16[112,1024]{1,0:T(8,128)(2,1)S(1)} %get-tuple-element.67), channel_id=1, source_target_pairs={{8,16},{9,17},{10,18},{11,19},{12,20},{13,21},{14,22},{15,23}} | collective-permute-start | bytes 688136 | tf_op jit(solution)/shard_map/ppermute | solution.py:369
  37.9 17.5 %collective-permute-start.10 = (bf16[112,1024]{1,0:T(8,128)(2,1)S(1)}, bf16[112,1024]{1,0:T(8,128)(2,1)S(1)}, u32[]{:S(2)}, u32[]{:S(2)}) collective-permute-start(bf16[112,1024]{1,0:T(8,128)(2,1)S(1)} %get-tuple-element.66), channel_id=1, source_target_pairs={{16,24},{17,25},{18,26},{19,27},{20,28},{21,29},{22,30},{23,31}} | collective-permute-start | bytes 688136 | tf_op jit(solution)/shard_map/ppermute | solution.py:369
  39.2 21.3 %collective-permute-start.8 = (bf16[112,1024]{1,0:T(8,128)(2,1)S(1)}, bf16[112,1024]{1,0:T(8,128)(2,1)S(1)}, u32[]{:S(2)}, u32[]{:S(2)}) collective-permute-start(bf16[112,1024]{1,0:T(8,128)(2,1)S(1)} %get-tuple-element.64), channel_id=1, source_target_pairs={{16,24},{17,25},{18,26},{19,27},{20,28},{21,29},{22,30},{23,31}} | collective-permute-start | bytes 688136 | tf_op jit(solution)/shard_map/ppermute | solution.py:369
  40.5 15.1 %collective-permute-start.9 = (bf16[96,1024]{1,0:T(8,128)(2,1)S(1)}, bf16[96,1024]{1,0:T(8,128)(2,1)S(1)}, u32[]{:S(2)}, u32[]{:S(2)}) collective-permute-start(bf16[96,1024]{1,0:T(8,128)(2,1)S(1)} %get-tuple-element.65), channel_id=1, source_target_pairs={{8,16},{9,17},{10,18},{11,19},{12,20},{13,21},{14,22},{15,23}} | collective-permute-start | bytes 589832 | tf_op jit(solution)/shard_map/ppermute | solution.py:369
  41.3 19.5 %collective-permute-start.7 = (bf16[80,1024]{1,0:T(8,128)(2,1)S(1)}, bf16[80,1024]{1,0:T(8,128)(2,1)S(1)}, u32[]{:S(2)}, u32[]{:S(2)}) collective-permute-start(bf16[80,1024]{1,0:T(8,128)(2,1)S(1)} %get-tuple-element.63), channel_id=1, source_target_pairs={{8,16},{9,17},{10,18},{11,19},{12,20},{13,21},{14,22},{15,23}} | collective-permute-start | bytes 491528 | tf_op jit(solution)/shard_map/ppermute | solution.py:369
  42.0 24.3 %collective-permute-start.14 = (bf16[112,1024]{1,0:T(8,128)(2,1)S(1)}, bf16[112,1024]{1,0:T(8,128)(2,1)S(1)}, u32[]{:S(2)}, u32[]{:S(2)}) collective-permute-start(bf16[112,1024]{1,0:T(8,128)(2,1)S(1)} %get-tuple-element.73), channel_id=1, source_target_pairs={{16,24},{17,25},{18,26},{19,27},{20,28},{21,29},{22,30},{23,31}} | collective-permute-start | bytes 688136 | tf_op jit(solution)/shard_map/ppermute | solution.py:369
  55.7 15.8 %collective-permute-start.13 = (bf16[96,1024]{1,0:T(8,128)(2,1)S(1)}, bf16[96,1024]{1,0:T(8,128)(2,1)S(1)}, u32[]{:S(2)}, u32[]{:S(2)}) collective-permute-start(bf16[96,1024]{1,0:T(8,128)(2,1)S(1)} %get-tuple-element.72), channel_id=1, source_target_pairs={{16,24},{17,25},{18,26},{19,27},{20,28},{21,29},{22,30},{23,31}} | collective-permute-start | bytes 589832 | tf_op jit(solution)/shard_map/ppermute | solution.py:369
  60.8 12.5 %collective-permute-start.12 = (bf16[80,1024]{1,0:T(8,128)(2,1)S(1)}, bf16[80,1024]{1,0:T(8,128)(2,1)S(1)}, u32[]{:S(2)}, u32[]{:S(2)}) collective-permute-start(bf16[80,1024]{1,0:T(8,128)(2,1)S(1)} %get-tuple-element.71), channel_id=1, source_target_pairs={{16,24},{17,25},{18,26},{19,27},{20,28},{21,29},{22,30},{23,31}} | collective-permute-start | bytes 491528 | tf_op jit(solution)/shard_map/ppermute | solution.py:369
